TPU v7x, 32 devices: a whole 2x2x4 slice. The times are simulated.
32 devices in a mesh: groups: 2 (over y), cache: 4 (over z), tensor: 4 (over x, core).
Axes of the slice: x: 2, y: 2, z: 4, core: 2. Of those that a mesh axis runs over, the one named last changes fastest.
Arguments:
- question_q: bfloat16 [16, 128, 8192], P(('groups', 'cache'), None, 'tensor'), parts along dimension 0, may hold values from -16 to 16
- question_kv: bfloat16 [16, 128, 8, 256], P(('groups', 'cache'), None, 'tensor'), parts along dimension 0, may hold values from -16 to 16
- passage_kv: bfloat16 [128, 8, 512, 256], P(('groups', 'cache'), 'tensor'), parts along dimension 0, may hold values from -6 to 6
- passage_ids: int32 [16, 8], P(('groups', 'cache')), parts along dimension 0, may hold values from 0 to 63, as said below
- passage_home: int32 [128], P('groups'), parts along dimension 0, may hold values from 0 to 63, as said below
- passage_offsets: int32 [16, 8], P(('groups', 'cache')), parts along dimension 0, may hold values from 0 to 3584, as said below
- out_weight: bfloat16 [8192, 8192], P('tensor', 'cache'), may hold values from -0.75 to 0.75
Outputs:
- mixed: bfloat16 [16, 128, 8192], P(('groups', 'cache'), None, 'tensor'), parts along dimension 0
There are 2 independent parts, one for each index of `groups`. A program takes and returns all parts, laid end to end along the dimension named above; an argument that names none is the same for every part. Nothing has to cross between parts.
Inputs may be any that keep to these rules, and one draw needn't show every extreme that they name: `passage_ids`: the 16 ids of the requests of one cache index are distinct; at most 8 of them have their passage_home row on one cache index's shard of passage_kv, and one shard holds 8 of them for every cache index. A permutation: passage n is row passage_home[n] of passage_kv. `passage_offsets`: each row is 512 times a permutation of 0 to 7.
All inputs are finite; a program needn't handle non-finite values.
Results may differ from a plain program's by a relative error of at most 0.013.
Values may be sent and summed in bfloat16 or wider, within the bound.
A program may use at most 256 MiB of HBM per device.

v0:
```python
import math

import jax
import jax.numpy as jnp
from jax import lax
from jax.sharding import PartitionSpec as P


def frequencies(head_width):
    pair_index = jnp.arange(head_width // 2, dtype=jnp.float32)
    inverse = jnp.power(jnp.float32(500000.0), -2.0 * pair_index / head_width)
    wavelength = 2.0 * math.pi / inverse
    smooth = (8192.0 / wavelength - 1.0) / 3.0
    blended = (1.0 - smooth) * inverse / 8.0 + smooth * inverse
    return jnp.where(
        wavelength < 2048.0, inverse, jnp.where(wavelength > 8192.0, inverse / 8.0, blended)
    )


def rotate(values, angles):
    half_width = values.shape[-1] // 2
    lower_half = values[..., :half_width]
    upper_half = values[..., half_width:]
    cosine = jnp.cos(angles)
    sine_values = jnp.sin(angles)
    return jnp.concatenate(
        [
            lower_half * cosine - upper_half * sine_values,
            upper_half * cosine + lower_half * sine_values,
        ],
        axis=-1,
    )


def attend(query_rows, own_pairs, passages, offsets, inverse):
    head_width = passages.shape[-1] // 2
    length = query_rows.shape[0]
    groups = own_pairs.shape[1]
    passage_count = passages.shape[0]
    span_tokens = passages.shape[2]
    positions = (passage_count * span_tokens + jnp.arange(length)).astype(jnp.float32)
    query_angles = positions[:, None] * inverse[None, :]
    queries = rotate(
        query_rows.reshape(length, groups, -1, head_width).astype(jnp.float32),
        query_angles[:, None, None, :],
    ).astype(jnp.bfloat16)
    own_keys = rotate(
        own_pairs[..., :head_width].astype(jnp.float32), query_angles[:, None, :]
    ).astype(jnp.bfloat16)
    own_values = own_pairs[..., head_width:]
    far_angles = offsets.astype(jnp.float32)[:, None] * inverse[None, :]
    far_keys = rotate(
        passages[..., :head_width].astype(jnp.float32), far_angles[:, None, None, :]
    ).astype(jnp.bfloat16)
    far_values = passages[..., head_width:]
    score_scale = 1.0 / math.sqrt(head_width)
    heads_per = queries.shape[2]
    far_scores = jnp.einsum(
        "tghd,ngpd->ghtnp", queries, far_keys, preferred_element_type=jnp.float32
    )
    far_scores = (
        far_scores.reshape(groups, heads_per, length, passage_count * span_tokens) * score_scale
    )
    own_scores = (
        jnp.einsum("tghd,sgd->ghts", queries, own_keys, preferred_element_type=jnp.float32)
        * score_scale
    )
    causal = jnp.arange(length)[:, None] >= jnp.arange(length)[None, :]
    own_scores = jnp.where(causal, own_scores, -jnp.inf)
    scores = jnp.concatenate([far_scores, own_scores], axis=-1)
    row_top = jnp.max(scores, axis=-1, keepdims=True)
    exponent = jnp.exp(scores - row_top)
    weights = (exponent / jnp.sum(exponent, axis=-1, keepdims=True)).astype(jnp.bfloat16)
    far_weights = weights[..., : passage_count * span_tokens].reshape(
        groups, heads_per, length, passage_count, span_tokens
    )
    own_weights = weights[..., passage_count * span_tokens :]
    result = jnp.einsum(
        "ghtnp,ngpd->tghd", far_weights, far_values, preferred_element_type=jnp.float32
    )
    result = result + jnp.einsum(
        "ghts,sgd->tghd", own_weights, own_values, preferred_element_type=jnp.float32
    )
    return result.astype(jnp.bfloat16).reshape(length, -1)


def local(
    question_q, question_kv, passage_kv, passage_ids, passage_home, passage_offsets, out_weight
):
    cache_count = lax.axis_size("cache")
    requests_here = passage_ids.shape[0]
    listed_count = passage_ids.shape[1]
    pick_count = requests_here * listed_count
    capacity = min(pick_count, max(2, (2 * pick_count + cache_count - 1) // cache_count))
    stored = passage_kv.shape[0]
    wanted = jnp.take(passage_home, passage_ids.reshape(pick_count), axis=0)
    owner_index = wanted // stored
    local_row = wanted % stored
    owner_hits = (owner_index[:, None] == jnp.arange(cache_count, dtype=jnp.int32)[None, :]).astype(
        jnp.int32
    )
    earlier = jnp.cumsum(owner_hits, axis=0) - owner_hits
    slot_rank = jnp.sum(earlier * owner_hits, axis=1)
    position = owner_index * capacity + slot_rank
    places = jnp.arange(cache_count * capacity, dtype=jnp.int32)
    slot_table = jnp.sum(
        jnp.where(position[:, None] == places[None, :], local_row[:, None], 0), axis=0
    )
    slot_table = slot_table.reshape(cache_count, capacity)
    served = jnp.take(
        passage_kv,
        lax.all_to_all(slot_table, "cache", split_axis=0, concat_axis=0, tiled=True),
        axis=0,
    )
    fetched = lax.all_to_all(served, "cache", split_axis=0, concat_axis=0, tiled=True)
    fetched = fetched.reshape((cache_count * capacity,) + passage_kv.shape[1:])
    picked = jnp.take(fetched, position, axis=0).reshape(
        (requests_here, listed_count) + passage_kv.shape[1:]
    )
    inverse = frequencies(passage_kv.shape[-1] // 2)

    def one_request(request_items):
        query_rows, own_pairs, passages, offsets = request_items
        return attend(query_rows, own_pairs, passages, offsets, inverse)

    attended = lax.map(one_request, (question_q, question_kv, picked, passage_offsets))
    token_block = attended.reshape(-1, attended.shape[-1])
    partial_terms = jnp.dot(
        token_block,
        lax.all_gather(out_weight, "cache", axis=1, tiled=True),
        preferred_element_type=jnp.float32,
    )
    mixed = lax.psum_scatter(
        partial_terms.astype(jnp.bfloat16), "tensor", scatter_dimension=1, tiled=True
    )
    return mixed.reshape(requests_here, question_q.shape[1], -1)


def solution(mesh):
    in_specs = (
        P(("groups", "cache"), None, "tensor"),
        P(("groups", "cache"), None, "tensor", None),
        P(("groups", "cache"), "tensor", None, None),
        P(("groups", "cache"), None),
        P("groups"),
        P(("groups", "cache"), None),
        P("tensor", "cache"),
    )
    out_specs = P(("groups", "cache"), None, "tensor")
    return jax.shard_map(local, mesh=mesh, in_specs=in_specs, out_specs=out_specs, check_vma=False)
```

profile of v0, /device:TPU:2, one launch (start us, length us, event | category | flops | bytes accessed | tf_op | source)
XLA Modules:
  0.0 1251.9 jit_solution(3652180890029410995)
XLA Ops:
  9.3 10.2 all_to_all.20
  19.6 10.5 gather_fusion.1
  30.1 14.2 %broadcast_select_fusion = bf16[4,8,2,512,256]{4,3,2,1,0:T(8,128)(2,1)} fusion(bf16[4,8,2,512,256]{4,3,2,1,0:T(8,128)(2,1)} %bitcast.116, pred[4,8]{1,0:T(4,128)(4,1)S(1)} %compare_and_fusion), kind=kLoop, calls=%fused_computation.57 | loop fusion | flops 8388608 | bytes 33554464 | tf_op jit(solution)/shard_map/jit(_take)/select_n | solution.py:110
  52.4 787.7 %all-to-all-done.1 = bf16[4,8,2,512,256]{4,3,2,1,0:T(8,128)(2,1)} async-done(((bf16[4,8,2,512,256]{4,3,2,1,0:T(8,128)(2,1)}), bf16[4,8,2,512,256]{4,3,2,1,0:T(8,128)(2,1)}, u32[]{:S(2)}, u32[]{:S(2)}) %all-to-all-start.1) | async-done | bytes 16777248 | tf_op jit(solution)/shard_map/all_to_all | solution.py:115
  840.1 10.7 gather_fusion.2
  858.4 326.0 %while.12 = (s32[]{:T(128)}, bf16[2,128,2048]{2,1,0:T(8,128)(2,1)}, bf16[2,8,2,512,256]{4,3,2,1,0:T(8,128)(2,1)}, s32[2,8]{1,0:T(2,128)S(1)}, bf16[2,128,2048]{2...) while((s32[]{:T(128)}, bf16[2,128,2048]{2,1,0:T(8,128)(2,1)}, ...), condition=%wide.region_7.8_spmd.clone.clone, body=%wide.region_3.7_spmd.clone.clone.sunk | while | flops 4520728576 | bytes 545573440 | solution.py:126
  873.3 15.0 %multiply_reduce_fusion.2 = (f32[2,128,8]{1,2,0:T(8,128)S(1)}, f32[2,8,128,8,512]{2,4,1,3,0:T(8,128)}) fusion(bf16[128,2,8,64]{3,0,2,1:T(8,128)(2,1)S(1)} %get-tuple-element.219, bf16[128,2,8,64]{3,0,2,1:T(8,128)(2,1)S(1)} %get-tuple-element.220, bf16[8,2,512,64]{3,2,0,1:T(8,128)(2,1)} %get-tuple-element.226, ...), kind=kOutput, calls=%fused_computation.7.clone.1 | convolution fusion | flops 2169501696 | bytes 36184064 | tf_op jit(solution)/shard_map/while/body/eval_jaxpr/tghd,ngpd->ghtnp/dot_general | solution.py:58
  888.3 22.8 %copy.90 = f32[2,8,128,8,512]{2,4,3,1,0:T(8,128)} copy(f32[2,8,128,8,512]{2,4,1,3,0:T(8,128)} %get-tuple-element.228) | data formatting | bytes 67108864 | tf_op jit(solution)/shard_map/while/body/eval_jaxpr/mul | solution.py:62
  911.1 31.2 %copy.91 = f32[2,8,128,4096]{3,2,1,0:T(8,128)} copy(f32[2,8,128,4096]{2,3,1,0:T(8,128)} %bitcast.113) | data formatting | bytes 67108864 | tf_op jit(solution)/shard_map/while/body/eval_jaxpr/mul | solution.py:62
  944.3 15.1 %fusion.45 = f32[2,8,128]{2,1,0:T(8,128)S(1)} fusion(f32[2,8,128,128]{3,2,1,0:T(8,128)S(1)} %copy.89, f32[2,8,128,4096]{3,2,1,0:T(8,128)} %copy.91, f32[2,8,128]{2,1,0:T(8,128)S(1)} %bitcast_maximum_fusion.2), kind=kLoop, calls=%fused_computation.9.clone.1 | loop fusion | flops 25950208 | bytes 34619392 | tf_op jit(solution)/shard_map/while/body/eval_jaxpr/reduce_sum | solution.py:73
  964.5 10.0 divide_convert_fusion.2
  974.5 14.0 %slice.121 = bf16[2,8,128,4096]{3,2,1,0:T(8,128)(2,1)} slice(bf16[2,8,128,4224]{3,2,1,0:T(8,128)(2,1)} %divide_convert_fusion.2), slice={[0:2], [0:8], [0:128], [0:4096]} | slice | bytes 33554432 | tf_op jit(solution)/shard_map/while/body/eval_jaxpr/slice | solution.py:74
  988.6 21.2 %copy.92 = bf16[2,8,128,4096]{2,3,1,0:T(8,128)(2,1)} copy(bf16[2,8,128,4096]{3,2,1,0:T(8,128)(2,1)} %slice.121) | data formatting | bytes 33554432 | tf_op jit(solution)/shard_map/while/body/eval_jaxpr/slice | solution.py:74
  1009.8 9.0 fusion.46
  1036.3 15.0 %multiply_reduce_fusion.2 = (f32[2,128,8]{1,2,0:T(8,128)S(1)}, f32[2,8,128,8,512]{2,4,1,3,0:T(8,128)}) fusion(bf16[128,2,8,64]{3,0,2,1:T(8,128)(2,1)S(1)} %get-tuple-element.219, bf16[128,2,8,64]{3,0,2,1:T(8,128)(2,1)S(1)} %get-tuple-element.220, bf16[8,2,512,64]{3,2,0,1:T(8,128)(2,1)} %get-tuple-element.226, ...), kind=kOutput, calls=%fused_computation.7.clone.1 | convolution fusion | flops 2169501696 | bytes 36184064 | tf_op jit(solution)/shard_map/while/body/eval_jaxpr/tghd,ngpd->ghtnp/dot_general | solution.py:58
  1051.3 22.8 %copy.90 = f32[2,8,128,8,512]{2,4,3,1,0:T(8,128)} copy(f32[2,8,128,8,512]{2,4,1,3,0:T(8,128)} %get-tuple-element.228) | data formatting | bytes 67108864 | tf_op jit(solution)/shard_map/while/body/eval_jaxpr/mul | solution.py:62
  1074.1 31.2 %copy.91 = f32[2,8,128,4096]{3,2,1,0:T(8,128)} copy(f32[2,8,128,4096]{2,3,1,0:T(8,128)} %bitcast.113) | data formatting | bytes 67108864 | tf_op jit(solution)/shard_map/while/body/eval_jaxpr/mul | solution.py:62
  1107.3 15.1 %fusion.45 = f32[2,8,128]{2,1,0:T(8,128)S(1)} fusion(f32[2,8,128,128]{3,2,1,0:T(8,128)S(1)} %copy.89, f32[2,8,128,4096]{3,2,1,0:T(8,128)} %copy.91, f32[2,8,128]{2,1,0:T(8,128)S(1)} %bitcast_maximum_fusion.2), kind=kLoop, calls=%fused_computation.9.clone.1 | loop fusion | flops 25950208 | bytes 34619392 | tf_op jit(solution)/shard_map/while/body/eval_jaxpr/reduce_sum | solution.py:73
  1127.6 10.0 divide_convert_fusion.2
  1137.5 14.0 %slice.121 = bf16[2,8,128,4096]{3,2,1,0:T(8,128)(2,1)} slice(bf16[2,8,128,4224]{3,2,1,0:T(8,128)(2,1)} %divide_convert_fusion.2), slice={[0:2], [0:8], [0:128], [0:4096]} | slice | bytes 33554432 | tf_op jit(solution)/shard_map/while/body/eval_jaxpr/slice | solution.py:74
  1151.6 21.2 %copy.92 = bf16[2,8,128,4096]{2,3,1,0:T(8,128)(2,1)} copy(bf16[2,8,128,4096]{3,2,1,0:T(8,128)(2,1)} %slice.121) | data formatting | bytes 33554432 | tf_op jit(solution)/shard_map/while/body/eval_jaxpr/slice | solution.py:74
  1172.8 9.0 fusion.46
  1184.5 16.7 %convolution_convert_fusion = bf16[256,8192]{1,0:T(8,128)(2,1)} fusion(bf16[256,2048]{1,0:T(8,128)(2,1)} %bitcast.124, bf16[2048,8192]{1,0:T(8,128)(2,1)} %all-gather.2.cloned.1.call-done), kind=kOutput, calls=%fused_computation.58 | convolution fusion | flops 8592031744 | bytes 38797312 | tf_op jit(solution)/shard_map/dot_general | solution.py:128
  1201.2 43.9 %reduce-scatter.2.cloned.1.call-done = bf16[256,2048]{1,0:T(8,128)(2,1)} async-done(((bf16[256,8192]{1,0:T(8,128)(2,1)}), bf16[256,2048]{1,0:T(8,128)(2,1)}) %reduce-scatter.2.cloned.1.call-update) | async-done | bytes 1048592 | tf_op jit(solution)/shard_map/reduce_scatter | solution.py:133
  (107 shorter events, 67.6 us)
Async XLA Ops:
  6.5 1.5 copy-start
  44.3 795.8 %all-to-all-start.1 = ((bf16[4,8,2,512,256]{4,3,2,1,0:T(8,128)(2,1)}), bf16[4,8,2,512,256]{4,3,2,1,0:T(8,128)(2,1)}, u32[]{:S(2)}, u32[]{:S(2)}) async-start(bf16[4,8,2,512,256]{4,3,2,1,0:T(8,128)(2,1)} %broadcast_select_fusion), calls=%async_computation.1 | async-start | bytes 33554432 | tf_op jit(solution)/shard_map/all_to_all | solution.py:115
  51.4 1.0 copy-start.5
  51.4 1133.1 %all-gather.2.cloned.1.call-start = ((), (), s32[]{:S(2)}) async-start(), calls=%async_computation.3 | async-start | bytes 41943040 | tf_op jit(solution)/shard_map/all_gather | solution.py:130
  52.1 1192.9 %reduce-scatter.2.cloned.1.call-start = ((), (), s32[]{:S(2)}) async-start(), calls=%async_computation.4 | async-start | bytes 5242880 | tf_op jit(solution)/shard_map/reduce_scatter | solution.py:133
  850.8 7.6 copy-start.8
  861.1 1.9 copy-start.3
  863.0 3.2 copy-start.4
  944.3 20.2 %copy-start.2 = (f32[2,8,128,4096]{3,2,1,0:T(8,128)S(1)}, f32[2,8,128,4096]{3,2,1,0:T(8,128)}, u32[]{:S(2)}) copy-start(f32[2,8,128,4096]{3,2,1,0:T(8,128)} %copy.91) | copy-start | bytes 100663296 | tf_op jit(solution)/shard_map/while
  1009.8 10.6 copy-start.6
  1020.5 1.0 copy-start.7
  1024.1 1.9 copy-start.3
  1026.0 3.2 copy-start.4
  1107.3 20.2 %copy-start.2 = (f32[2,8,128,4096]{3,2,1,0:T(8,128)S(1)}, f32[2,8,128,4096]{3,2,1,0:T(8,128)}, u32[]{:S(2)}) copy-start(f32[2,8,128,4096]{3,2,1,0:T(8,128)} %copy.91) | copy-start | bytes 100663296 | tf_op jit(solution)/shard_map/while
  1172.8 10.6 copy-start.6
  1183.5 1.0 copy-start.7
  1184.5 60.6 %copy-start.1 = (s32[64]{0:T(128)S(1)}, s32[64]{0:T(128)}, u32[]{:S(2)}) copy-start(s32[64]{0:T(128)} %param.13) | copy-start | bytes 772
Sparse Core Ops, SparseCore 0:
  53.8 898.8 all-gather.1
  1201.3 43.7 reduce-scatter.1
where the time goes:
time: 1260 us; the launch traced here: 1250 us
  waiting for transfers between devices  832 us (66%)
  local copies, waits for them, and re-layouts  236 us (19%)
  other arithmetic  83.7 us (7%)
  matrix products  68.3 us (5%)
  between operations  13.5 us (1%)
    all_to_all x1, waiting for transfers between devices, local(): lax.all_to_all(served, 'cache', split_axis=0, concat_axis=0, tiled=True)  788 us
    mul x4, local copies, waits for them, and re-layouts, attend(): far_scores.reshape(groups, heads_per, length, passage_count * span_tokens)  108 us
    slice x4, local copies, waits for them, and re-layouts, attend(): weights[..., :passage_count * span_tokens]  70.5 us
    reduce_scatter x1, waiting for transfers between devices, local(): lax.psum_scatter(partial_terms.astype(jnp.bfloat16), 'tensor', scatter_di...  43.9 us
    reduce_sum x2, other arithmetic, attend(): jnp.sum(exponent, axis=-1, keepdims=True)  30.2 us
    dot_general x2, matrix products, attend(): jnp.einsum('tghd,ngpd->ghtnp', queries, far_keys, preferred_element_type=...  29.9 us
  transfers between devices with their start and end apart: 3, of which 2 were waited for; matrix products, arithmetic and copies ran while one was open for 26% of the time, Pallas kernels for 0%

commit v1 on v0

v1 whole, which is shorter than its diff:
```python
import functools
import math

import jax
import jax.numpy as jnp
from jax import lax
from jax.experimental import pallas as pl
from jax.experimental.pallas import tpu as pltpu
from jax.sharding import PartitionSpec as P

LOW = -1e30


def frequencies(head_width):
    pair_index = jnp.arange(head_width // 2, dtype=jnp.float32)
    inverse = jnp.power(jnp.float32(500000.0), -2.0 * pair_index / head_width)
    wavelength = 2.0 * math.pi / inverse
    smooth = (8192.0 / wavelength - 1.0) / 3.0
    blended = (1.0 - smooth) * inverse / 8.0 + smooth * inverse
    return jnp.where(
        wavelength < 2048.0, inverse, jnp.where(wavelength > 8192.0, inverse / 8.0, blended)
    )


def tables(positions, inverse):
    angles = positions.astype(jnp.float32)[:, None] * inverse[None, :]
    cosine, sine = jnp.cos(angles), jnp.sin(angles)
    return jnp.concatenate([cosine, cosine], 1), jnp.concatenate([-sine, sine], 1)


def turn(x, cosine, sine):
    return x * cosine + pltpu.roll(x, x.shape[1] // 2, 1) * sine


def fold(q, keys, values, masked, m_ref, acc_ref, rows, first):
    s = lax.dot_general(q, keys, (((1,), (1,)), ((), ())), preferred_element_type=jnp.float32)
    if masked is not None:
        s = jnp.where(masked, s, LOW)
    top = jnp.max(s, axis=1, keepdims=True)
    width = values.shape[1] // 2
    if first:
        new = jnp.broadcast_to(top, (s.shape[0], width))
    else:
        old = m_ref[rows, :]
        new = jnp.maximum(old, top)
    wide = new if s.shape[1] == width else jnp.concatenate([new] * (s.shape[1] // width), 1)
    p = jnp.exp2(s - wide).astype(jnp.bfloat16)
    pv = jnp.dot(p, values, preferred_element_type=jnp.float32)
    if not first:
        alpha = jnp.exp2(old - new)
        pv = acc_ref[rows, :] * jnp.concatenate([alpha, alpha], 1) + pv
    acc_ref[rows, :] = pv
    m_ref[rows, :] = new


def attend_kernel(
    listed, scale, me_ref, ids, home, q, kv, own, cq, sq, cf, sf, o, lse, qs, acc, m
):
    request = pl.program_id(0)
    stored, groups, span, both = kv.shape
    width = both // 2
    length = q.shape[1]
    heads = q.shape[2] // width
    per = heads // groups
    step = min(2, per)
    mine = me_ref[0]
    here = own.shape[0]
    ones = jnp.ones((span, width), jnp.bfloat16)
    for h in range(heads):
        x = q[0, :, h * width : (h + 1) * width].astype(jnp.float32)
        qs[h * length : (h + 1) * length, :] = (
            turn(x, cq[...], sq[...]) * scale
        ).astype(jnp.bfloat16)
    chunk = step * length

    @pl.when(request // here == mine)
    def _():
        r = request - mine * here
        at = lax.broadcasted_iota(jnp.int32, (chunk, length), 0) % length
        causal = at >= lax.broadcasted_iota(jnp.int32, (chunk, length), 1)
        for g in range(groups):
            pair = own[r, g]
            keys = turn(pair[:, :width].astype(jnp.float32), cq[...], sq[...])
            keys = keys.astype(jnp.bfloat16)
            values = jnp.concatenate([pair[:, width:], ones[:length]], 1)
            for i in range(per // step):
                rows = pl.ds((g * per + i * step) * length, chunk)
                fold(qs[rows, :], keys, values, causal, m, acc, rows, True)

    @pl.when(request // here != mine)
    def _():
        m[...] = jnp.full_like(m, LOW)
        acc[...] = jnp.zeros_like(acc)

    def slot(j, carry):
        at = request * listed + j
        row = home[ids[at]]

        @pl.when(row // stored == mine)
        def _():
            local = row - mine * stored
            cosine, sine = cf[pl.ds(at, 1), :], sf[pl.ds(at, 1), :]
            for g in range(groups):
                pair = kv[local, g]
                keys = turn(pair[:, :width].astype(jnp.float32), cosine, sine)
                keys = keys.astype(jnp.bfloat16)
                values = jnp.concatenate([pair[:, width:], ones], 1)
                for i in range(per // step):
                    rows = pl.ds((g * per + i * step) * length, chunk)
                    fold(qs[rows, :], keys, values, None, m, acc, rows, False)

        return carry

    lax.fori_loop(0, listed, slot, 0)
    eye = lax.broadcasted_iota(jnp.int32, (length, width), 0) == lax.broadcasted_iota(
        jnp.int32, (length, width), 1
    )
    for h in range(heads):
        rows = pl.ds(h * length, length)
        total = acc[rows, width:]
        some = total > 0.0
        safe = jnp.where(some, total, 1.0)
        o[0, :, h * width : (h + 1) * width] = (acc[rows, :width] / safe).astype(jnp.bfloat16)
        level = jnp.where(some, m[rows, :] + jnp.log2(safe), LOW)
        lse[0, h : h + 1, :] = jnp.sum(jnp.where(eye, level, 0.0), axis=0, keepdims=True)


def attend(me, ids, home, q, kv, own, cq, sq, cf, sf):
    requests, length, span = q.shape
    groups, both = kv.shape[1], kv.shape[3]
    width = both // 2
    heads = span // width
    whole = lambda a: pl.BlockSpec(a.shape, lambda i: (0,) * a.ndim, pipeline_mode=pl.Buffered(1))
    smem = pl.BlockSpec(memory_space=pltpu.SMEM)
    return pl.pallas_call(
        functools.partial(
            attend_kernel, ids.shape[0] // requests, math.log2(math.e) / math.sqrt(width)
        ),
        grid=(requests,),
        in_specs=[
            smem,
            smem,
            smem,
            pl.BlockSpec((1, length, span), lambda i: (i, 0, 0)),
            whole(kv),
            whole(own),
            whole(cq),
            whole(sq),
            whole(cf),
            whole(sf),
        ],
        out_specs=[
            pl.BlockSpec((1, length, span), lambda i: (i, 0, 0)),
            pl.BlockSpec((1, heads, length), lambda i: (i, 0, 0)),
        ],
        out_shape=[
            jax.ShapeDtypeStruct((requests, length, span), jnp.bfloat16),
            jax.ShapeDtypeStruct((requests, heads, length), jnp.float32),
        ],
        scratch_shapes=[
            pltpu.VMEM((heads * length, width), jnp.bfloat16),
            pltpu.VMEM((heads * length, 2 * width), jnp.float32),
            pltpu.VMEM((heads * length, width), jnp.float32),
        ],
        compiler_params=pltpu.CompilerParams(vmem_limit_bytes=40 * 1024 * 1024),
    )(me, ids, home, q, kv, own, cq, sq, cf, sf)


def merge_kernel(o, lse, out):
    count, _, heads, length = lse.shape
    width = o.shape[3] // heads
    levels = [lse[c, 0] for c in range(count)]
    top = functools.reduce(jnp.maximum, levels)
    shares = [jnp.exp2(level - top) for level in levels]
    total = functools.reduce(jnp.add, shares)
    shares = [share / total for share in shares]
    for h in range(heads):
        at = slice(h * width, (h + 1) * width)
        result = jnp.zeros((length, width), jnp.float32)
        for c in range(count):
            column = jnp.transpose(jnp.broadcast_to(shares[c][h : h + 1, :], (width, length)))
            result += o[c, 0, :, at].astype(jnp.float32) * column
        out[0, :, at] = result.astype(jnp.bfloat16)


def merge(o, lse):
    count, requests, length, span = o.shape
    heads = lse.shape[2]
    return pl.pallas_call(
        merge_kernel,
        grid=(requests,),
        in_specs=[
            pl.BlockSpec((count, 1, length, span), lambda i: (0, i, 0, 0)),
            pl.BlockSpec((count, 1, heads, length), lambda i: (0, i, 0, 0)),
        ],
        out_specs=pl.BlockSpec((1, length, span), lambda i: (i, 0, 0)),
        out_shape=jax.ShapeDtypeStruct((requests, length, span), jnp.bfloat16),
        compiler_params=pltpu.CompilerParams(vmem_limit_bytes=40 * 1024 * 1024),
    )(o, lse)


def local(
    question_q, question_kv, passage_kv, passage_ids, passage_home, passage_offsets, out_weight
):
    caches, tensors = lax.axis_size("cache"), lax.axis_size("tensor")
    me_cache, me_tensor = lax.axis_index("cache"), lax.axis_index("tensor")
    here, length, span = question_q.shape
    width = passage_kv.shape[-1] // 2
    listed = passage_ids.shape[1]
    inverse = frequencies(width)
    lists = lax.all_gather(
        jnp.stack([passage_ids, passage_offsets]), "cache", axis=1, tiled=True
    )
    ids, offsets = lists[0].reshape(-1), lists[1].reshape(-1)
    q_all = lax.all_gather(question_q, "cache", axis=0, tiled=True)
    cq, sq = tables(listed * passage_kv.shape[2] + jnp.arange(length), inverse)
    cf, sf = tables(offsets, inverse)
    own = jnp.swapaxes(question_kv, 1, 2)
    o, lse = attend(
        me_cache.reshape(1).astype(jnp.int32), ids, passage_home, q_all, passage_kv, own,
        cq, sq, cf, sf,
    )
    o = lax.all_to_all(o, "cache", split_axis=0, concat_axis=0, tiled=True)
    lse = lax.all_to_all(lse, "cache", split_axis=0, concat_axis=0, tiled=True)
    attended = merge(
        o.reshape((caches, here, length, span)), lse.reshape((caches, here) + lse.shape[1:])
    )
    rows = lax.all_gather(attended.reshape(here * length, span), "cache", axis=0, tiled=True)
    partial = jnp.dot(rows, out_weight, preferred_element_type=jnp.float32)
    summed = lax.psum_scatter(
        partial.astype(jnp.bfloat16), "tensor", scatter_dimension=0, tiled=True
    )
    fan = caches // tensors
    tokens = here * length
    columns = out_weight.shape[1]
    blocks = summed.reshape(fan, tokens, columns)
    pieces = []
    for turn_at in range(fan):
        pairs = []
        for c in range(caches):
            for t in range(tensors):
                to = (t * fan + (turn_at + c % fan) % fan, c // fan)
                pairs.append((c * tensors + t, to[0] * tensors + to[1]))
        block = blocks[0]
        if fan > 1:
            block = lax.dynamic_index_in_dim(blocks, (turn_at + me_cache) % fan, 0, False)
        pieces.append(lax.ppermute(block, ("cache", "tensor"), pairs))
    if fan == 1:
        mixed = pieces[0]
    else:
        stacked = jnp.stack(pieces)
        order = (me_cache - jnp.arange(fan)) % fan
        mixed = jnp.take(stacked, order, axis=0)
        mixed = jnp.swapaxes(mixed, 0, 1).reshape(tokens, fan * columns)
    return mixed.reshape(here, length, -1)


def solution(mesh):
    in_specs = (
        P(("groups", "cache"), None, "tensor"),
        P(("groups", "cache"), None, "tensor", None),
        P(("groups", "cache"), "tensor", None, None),
        P(("groups", "cache"), None),
        P("groups"),
        P(("groups", "cache"), None),
        P("tensor", "cache"),
    )
    out_specs = P(("groups", "cache"), None, "tensor")
    return jax.shard_map(local, mesh=mesh, in_specs=in_specs, out_specs=out_specs, check_vma=False)
```

time: 1260 us -> 466 us (0.37)
  waiting for transfers between devices: 832 us -> 238 us
  local copies, waits for them, and re-layouts: 236 us -> 4.99 us
  blocking collectives: 10.2 us -> 154 us
  other arithmetic: 83.7 us -> 1.43 us
  matrix products: 68.3 us -> 13.8 us
  Pallas kernels: 0 us -> 33.7 us
    all_to_all x1 -> x0, waiting for transfers between devices: 788 us -> none  [local(): lax.all_to_all(served, 'cache', split_axis=0, concat_axis=0, tiled=True)]
    all_gather x1 -> x2, waiting for transfers between devices: 0.01 us -> 149 us  [the longest x1 79.9 us: local(): lax.all_gather(attended.reshape(here * length, span), 'cache', axis=0, ti...]
    all_to_all x1 -> x2, blocking collectives: 10.2 us -> 142 us  [the longest x1 94.5 us: local(): o = lax.all_to_all(o, 'cache', split_axis=0, concat_axis=0, tiled=True)]
    mul x4 -> x0, local copies, waits for them, and re-layouts: 108 us -> none  [attend(): far_scores.reshape(groups, heads_per, length, passage_count * span_tokens)]
    slice x6 -> x1, local copies, waits for them, and re-layouts: 72.3 us -> 0.02 us  [local(): ids, offsets = (lists[0].reshape(-1), lists[1].reshape(-1))]
    dot_general x9 -> x1, matrix products: 68.3 us -> 13.8 us  [local(): partial = jnp.dot(rows, out_weight, preferred_element_type=jnp.float32)]
    ppermute x0 -> x1, waiting for transfers between devices: none -> 46.6 us  [local(): pieces.append(lax.ppermute(block, ('cache', 'tensor'), pairs))]
    pallas_call x0 -> x2, Pallas kernels: none -> 33.7 us  [the longest x1 30.2 us: attend(): pl.pallas_call(functools.partial(attend_kernel, ids.shape[0] // requests,...]
  transfers between devices with their start and end apart: 3 -> 4, of which waited for: 2 -> 4; matrix products, arithmetic and copies ran while one was open for 26% -> 1% of each run, Pallas kernels for 0% -> 0%
where the time goes in v1:
time: 466 us; the launch traced here: 465 us
  waiting for transfers between devices  238 us (51%)
  blocking collectives  154 us (33%)
  Pallas kernels  33.7 us (7%)
  matrix products  13.8 us (3%)
  between operations  13.2 us (3%)
  starting transfers between devices  5.51 us (1%)
  local copies, waits for them, and re-layouts  4.99 us (1%)
    all_to_all x1, blocking collectives, local(): o = lax.all_to_all(o, 'cache', split_axis=0, concat_axis=0, tiled=True)  94.5 us
    all_gather x1, waiting for transfers between devices, local(): lax.all_gather(attended.reshape(here * length, span), 'cache', axis=0, ti...  79.9 us
    all_gather x1, waiting for transfers between devices, local(): q_all = lax.all_gather(question_q, 'cache', axis=0, tiled=True)  68.9 us
    all_to_all x1, blocking collectives, local(): lse = lax.all_to_all(lse, 'cache', split_axis=0, concat_axis=0, tiled=True)  47.7 us
    ppermute x1, waiting for transfers between devices, local(): pieces.append(lax.ppermute(block, ('cache', 'tensor'), pairs))  46.6 us
    reduce_scatter x1, waiting for transfers between devices, local(): lax.psum_scatter(partial.astype(jnp.bfloat16), 'tensor', scatter_dimensio...  42 us
    pallas_call x1, Pallas kernels, attend(): pl.pallas_call(functools.partial(attend_kernel, ids.shape[0] // requests,...  30.2 us
    dot_general x1, matrix products, local(): partial = jnp.dot(rows, out_weight, preferred_element_type=jnp.float32)  13.8 us
  transfers between devices with their start and end apart: 4, of which 4 were waited for; matrix products, arithmetic and copies ran while one was open for 1% of the time, Pallas kernels for 0%

profile of v1, /device:TPU:2, one launch (start us, length us, event | category | flops | bytes accessed | tf_op | source)
XLA Modules:
  0.0 465.2 jit_solution(7607011446759665086)
XLA Ops:
  6.5 0.7 all-gather.3.cloned.1.call-update
  7.3 0.7 pad_add_fusion
  8.0 12.1 %all_gather.9 = s32[2,8,8]{2,0,1:T(2,128)S(1)} all-gather(s32[2,2,8]{2,0,1:T(2,128)S(1)} %copy.9), channel_id=1, replica_groups=mesh['groups'=2,'cache'=4,'tensor'=4] {'cache'}, dimensions={1}, use_global_device_ids=true | all-gather | bytes 640 | tf_op jit(solution)/shard_map/all_gather | solution.py:211
  20.1 0.1 reshape_squeeze.4.ids
  20.2 0.1 convert_element_type.28
  20.3 1.0 copy.12
  21.3 0.2 fusion.1
  21.5 0.1 pad_maximum_fusion.2
  21.6 0.3 fusion
  22.0 0.1 pad_maximum_fusion
  22.1 68.9 %all-gather.3.cloned.1.call-done.q = bf16[8,128,2048]{2,1,0:T(8,128)(2,1)} async-done(((bf16[2,128,2048]{2,1,0:T(8,128)(2,1)}), bf16[8,128,2048]{2,1,0:T(8,128)(2,1)}) %all-gather.3.cloned.1.call-update) | async-done | bytes 4194320 | tf_op jit(solution)/shard_map/all_gather | solution.py:215
  91.0 2.2 copy-done
  93.2 0.7 copy-done.1
  93.8 30.2 %shard_map.73 = (bf16[8,128,2048]{2,1,0:T(8,128)(2,1)S(1)}, f32[8,16,128]{2,1,0:T(8,128)S(1)}) custom-call(s32[1]{0:T(128)} %bitcast.me_ref, s32[64]{0:T(128)S(1)} %reshape_squeeze.4.ids, s32[64]{0:T(128)S(1)} %copy-done.1, bf16[8,128,2048]{2,1,0:T(8,128)(2,1)S(1)} %copy-done, bf16[16,2,512,256]{3,2,1,0:T(8,128)(2,1)} %kv.1, ...), custom_call_target="tpu_custom_call" | custom-call | tf_op jit(solution)/shard_map/pallas_call | solution.py:135
  124.1 47.7 %all_to_all.10 = f32[8,16,128]{2,1,0:T(8,128)S(1)} all-to-all(f32[8,16,128]{2,1,0:T(8,128)S(1)} %get-tuple-element.8), channel_id=1, replica_groups=mesh['groups'=2,'cache'=4,'tensor'=4] {'cache'}, dimensions={0} | all-to-all | bytes 131072 | tf_op jit(solution)/shard_map/all_to_all | solution.py:224
  171.8 94.5 %all_to_all.11 = bf16[8,128,2048]{2,1,0:T(8,128)(2,1)S(1)} all-to-all(bf16[8,128,2048]{2,1,0:T(8,128)(2,1)S(1)} %get-tuple-element.7), channel_id=1, replica_groups=mesh['groups'=2,'cache'=4,'tensor'=4] {'cache'}, dimensions={0} | all-to-all | bytes 8388608 | tf_op jit(solution)/shard_map/all_to_all | solution.py:223
  266.3 3.4 shard_map.74
  269.8 0.0 reduce-scatter.2.cloned.1.call-start
  269.8 79.9 %all-gather.5.cloned.1.call-done = bf16[1024,2048]{1,0:T(8,128)(2,1)} async-done(((bf16[256,2048]{1,0:T(8,128)(2,1)}), bf16[1024,2048]{1,0:T(8,128)(2,1)}) %all-gather.5.cloned.1.call-update) | async-done | bytes 4194320 | tf_op jit(solution)/shard_map/all_gather | solution.py:228
  349.8 13.8 %convolution_convert_fusion = bf16[1024,2048]{1,0:T(8,128)(2,1)} fusion(bf16[1024,2048]{1,0:T(8,128)(2,1)} %all-gather.5.cloned.1.call-done, bf16[2048,2048]{1,0:T(8,128)(2,1)} %param.13), kind=kOutput, calls=%fused_computation | convolution fusion | flops 8592031744 | bytes 16777216 | tf_op jit(solution)/shard_map/dot_general | solution.py:229
  363.6 42.0 %reduce-scatter.2.cloned.1.call-done = bf16[256,2048]{1,0:T(8,128)(2,1)} async-done(((bf16[1024,2048]{1,0:T(8,128)(2,1)}), bf16[256,2048]{1,0:T(8,128)(2,1)}) %reduce-scatter.2.cloned.1.call-update) | async-done | bytes 1048592 | tf_op jit(solution)/shard_map/reduce_scatter | solution.py:230
  405.6 5.4 %collective-permute-start = (bf16[256,2048]{1,0:T(8,128)(2,1)}, bf16[256,2048]{1,0:T(8,128)(2,1)S(1)}, u32[]{:S(2)}, u32[]{:S(2)}) collective-permute-start(bf16[256,2048]{1,0:T(8,128)(2,1)} %reduce-scatter.2.cloned.1.call-done), channel_id=1, source_target_pairs={{0,0},{1,4},{2,8},{3,12},{4,1},{5,5},{6,9},{7,13},{8,2},{9,6},{10,... | collective-permute-start | bytes 3145736 | tf_op jit(solution)/shard_map/ppermute | solution.py:247
  411.0 46.6 %collective-permute-done = bf16[256,2048]{1,0:T(8,128)(2,1)S(1)} collective-permute-done((bf16[256,2048]{1,0:T(8,128)(2,1)}, bf16[256,2048]{1,0:T(8,128)(2,1)S(1)}, u32[]{:S(2)}, u32[]{:S(2)}) %collective-permute-start) | collective-permute-done | bytes 1048608 | tf_op jit(solution)/shard_map/ppermute | solution.py:247
  457.7 1.0 copy.14
  (11 shorter events, 0.1 us)
Async XLA Ops:
  6.5 84.5 %all-gather.3.cloned.1.call-start = ((), (), s32[]{:S(2)}) async-start(), calls=%async_computation.3 | async-start | bytes 5242880 | tf_op jit(solution)/shard_map/all_gather | solution.py:215
  7.3 342.5 %all-gather.5.cloned.1.call-start = ((), (), s32[]{:S(2)}) async-start(), calls=%async_computation.4 | async-start | bytes 5242880 | tf_op jit(solution)/shard_map/all_gather | solution.py:228
  91.0 2.2 copy-start
  93.2 0.7 copy-start.1
  269.8 135.8 %reduce-scatter.2.cloned.1.call-start = ((), (), s32[]{:S(2)}) async-start(), calls=%async_computation.5 | async-start | bytes 5242880 | tf_op jit(solution)/shard_map/reduce_scatter | solution.py:230
  405.6 52.1 %collective-permute-start = (bf16[256,2048]{1,0:T(8,128)(2,1)}, bf16[256,2048]{1,0:T(8,128)(2,1)S(1)}, u32[]{:S(2)}, u32[]{:S(2)}) collective-permute-start(bf16[256,2048]{1,0:T(8,128)(2,1)} %reduce-scatter.2.cloned.1.call-done), channel_id=1, source_target_pairs={{0,0},{1,4},{2,8},{3,12},{4,1},{5,5},{6,9},{7,13},{8,2},{9,6},{10,... | collective-permute-start | bytes 3145736 | tf_op jit(solution)/shard_map/ppermute | solution.py:247
Sparse Core Ops, SparseCore 0:
  8.9 82.0 all-gather.2
  269.9 79.8 all-gather.4
  363.7 41.8 reduce-scatter.1

commit v2 on v1

--- a/solution.py
+++ b/solution.py
@@ -9,6 +9,7 @@
 from jax.sharding import PartitionSpec as P
 
 LOW = -1e30
+EXTRA = 16
 
 
 def frequencies(head_width):
@@ -54,12 +55,12 @@
 
 
 def attend_kernel(
-    listed, scale, me_ref, ids, home, q, kv, own, cq, sq, cf, sf, o, lse, qs, acc, m
+    listed, scale, me_ref, ids, home, q, kv, own, cq, sq, cf, sf, o, qs, acc, m
 ):
     request = pl.program_id(0)
     stored, groups, span, both = kv.shape
     width = both // 2
-    length = q.shape[1]
+    length = own.shape[2]
     heads = q.shape[2] // width
     per = heads // groups
     step = min(2, per)
@@ -67,7 +68,7 @@
     here = own.shape[0]
     ones = jnp.ones((span, width), jnp.bfloat16)
     for h in range(heads):
-        x = q[0, :, h * width : (h + 1) * width].astype(jnp.float32)
+        x = q[0, :length, h * width : (h + 1) * width].astype(jnp.float32)
         qs[h * length : (h + 1) * length, :] = (
             turn(x, cq[...], sq[...]) * scale
         ).astype(jnp.bfloat16)
@@ -120,15 +121,22 @@
         total = acc[rows, width:]
         some = total > 0.0
         safe = jnp.where(some, total, 1.0)
-        o[0, :, h * width : (h + 1) * width] = (acc[rows, :width] / safe).astype(jnp.bfloat16)
+        at = slice(h * width, (h + 1) * width)
+        o[0, :length, at] = (acc[rows, :width] / safe).astype(jnp.bfloat16)
         level = jnp.where(some, m[rows, :] + jnp.log2(safe), LOW)
-        lse[0, h : h + 1, :] = jnp.sum(jnp.where(eye, level, 0.0), axis=0, keepdims=True)
+        level = jnp.sum(jnp.where(eye, level, 0.0), axis=0, keepdims=True)
+        high = level.astype(jnp.bfloat16).astype(jnp.float32)
+        middle = (level - high).astype(jnp.bfloat16).astype(jnp.float32)
+        low = level - high - middle
+        line = lax.broadcasted_iota(jnp.int32, (EXTRA, width), 0)
+        parts = jnp.where(line == 0, high, jnp.where(line == 1, middle, jnp.where(line == 2, low, 0.0)))
+        o[0, length:, at] = parts.astype(jnp.bfloat16)
 
 
 def attend(me, ids, home, q, kv, own, cq, sq, cf, sf):
-    requests, length, span = q.shape
-    groups, both = kv.shape[1], kv.shape[3]
-    width = both // 2
+    requests, rows, span = q.shape
+    length = own.shape[2]
+    width = kv.shape[3] // 2
     heads = span // width
     whole = lambda a: pl.BlockSpec(a.shape, lambda i: (0,) * a.ndim, pipeline_mode=pl.Buffered(1))
     smem = pl.BlockSpec(memory_space=pltpu.SMEM)
@@ -141,7 +149,7 @@
             smem,
             smem,
             smem,
-            pl.BlockSpec((1, length, span), lambda i: (i, 0, 0)),
+            pl.BlockSpec((1, rows, span), lambda i: (i, 0, 0)),
             whole(kv),
             whole(own),
             whole(cq),
@@ -149,54 +157,51 @@
             whole(cf),
             whole(sf),
         ],
-        out_specs=[
-            pl.BlockSpec((1, length, span), lambda i: (i, 0, 0)),
-            pl.BlockSpec((1, heads, length), lambda i: (i, 0, 0)),
-        ],
-        out_shape=[
-            jax.ShapeDtypeStruct((requests, length, span), jnp.bfloat16),
-            jax.ShapeDtypeStruct((requests, heads, length), jnp.float32),
-        ],
+        out_specs=pl.BlockSpec((1, rows, span), lambda i: (i, 0, 0)),
+        out_shape=jax.ShapeDtypeStruct((requests, rows, span), jnp.bfloat16),
         scratch_shapes=[
             pltpu.VMEM((heads * length, width), jnp.bfloat16),
             pltpu.VMEM((heads * length, 2 * width), jnp.float32),
             pltpu.VMEM((heads * length, width), jnp.float32),
         ],
         compiler_params=pltpu.CompilerParams(vmem_limit_bytes=40 * 1024 * 1024),
+        cost_estimate=pl.CostEstimate(
+            flops=requests * 4 * 4 * length * kv.shape[2] * span,
+            bytes_accessed=2 * (kv.size + 2 * q.size),
+            transcendentals=requests * 4 * heads * length * kv.shape[2],
+        ),
     )(me, ids, home, q, kv, own, cq, sq, cf, sf)
 
 
-def merge_kernel(o, lse, out):
-    count, _, heads, length = lse.shape
-    width = o.shape[3] // heads
-    levels = [lse[c, 0] for c in range(count)]
-    top = functools.reduce(jnp.maximum, levels)
-    shares = [jnp.exp2(level - top) for level in levels]
-    total = functools.reduce(jnp.add, shares)
-    shares = [share / total for share in shares]
+def merge_kernel(*refs):
+    out = refs[-1]
+    parts = refs[:-1]
+    length = out.shape[0]
+    width = length
+    heads = out.shape[1] // width
     for h in range(heads):
         at = slice(h * width, (h + 1) * width)
+        levels = []
+        for o in parts:
+            tail = o[length:, at].astype(jnp.float32)
+            levels.append(tail[0:1] + tail[1:2] + tail[2:3])
+        top = functools.reduce(jnp.maximum, levels)
+        shares = [jnp.exp2(level - top) for level in levels]
+        total = functools.reduce(jnp.add, shares)
         result = jnp.zeros((length, width), jnp.float32)
-        for c in range(count):
-            column = jnp.transpose(jnp.broadcast_to(shares[c][h : h + 1, :], (width, length)))
-            result += o[c, 0, :, at].astype(jnp.float32) * column
-        out[0, :, at] = result.astype(jnp.bfloat16)
-
-
-def merge(o, lse):
-    count, requests, length, span = o.shape
-    heads = lse.shape[2]
+        for o, share in zip(parts, shares):
+            column = jnp.transpose(jnp.broadcast_to(share / total, (width, length)))
+            result += o[:length, at].astype(jnp.float32) * column
+        out[:, at] = result.astype(jnp.bfloat16)
+
+
+def merge(parts, length):
+    rows, span = parts[0].shape
     return pl.pallas_call(
         merge_kernel,
-        grid=(requests,),
-        in_specs=[
-            pl.BlockSpec((count, 1, length, span), lambda i: (0, i, 0, 0)),
-            pl.BlockSpec((count, 1, heads, length), lambda i: (0, i, 0, 0)),
-        ],
-        out_specs=pl.BlockSpec((1, length, span), lambda i: (i, 0, 0)),
-        out_shape=jax.ShapeDtypeStruct((requests, length, span), jnp.bfloat16),
-        compiler_params=pltpu.CompilerParams(vmem_limit_bytes=40 * 1024 * 1024),
-    )(o, lse)
+        out_shape=jax.ShapeDtypeStruct((length, span), jnp.bfloat16),
+        compiler_params=pltpu.CompilerParams(vmem_limit_bytes=48 * 1024 * 1024),
+    )(*parts)
 
 
 def local(
@@ -208,31 +213,44 @@
     width = passage_kv.shape[-1] // 2
     listed = passage_ids.shape[1]
     inverse = frequencies(width)
-    lists = lax.all_gather(
-        jnp.stack([passage_ids, passage_offsets]), "cache", axis=1, tiled=True
-    )
-    ids, offsets = lists[0].reshape(-1), lists[1].reshape(-1)
-    q_all = lax.all_gather(question_q, "cache", axis=0, tiled=True)
     cq, sq = tables(listed * passage_kv.shape[2] + jnp.arange(length), inverse)
-    cf, sf = tables(offsets, inverse)
     own = jnp.swapaxes(question_kv, 1, 2)
-    o, lse = attend(
-        me_cache.reshape(1).astype(jnp.int32), ids, passage_home, q_all, passage_kv, own,
-        cq, sq, cf, sf,
-    )
-    o = lax.all_to_all(o, "cache", split_axis=0, concat_axis=0, tiled=True)
-    lse = lax.all_to_all(lse, "cache", split_axis=0, concat_axis=0, tiled=True)
-    attended = merge(
-        o.reshape((caches, here, length, span)), lse.reshape((caches, here) + lse.shape[1:])
-    )
-    rows = lax.all_gather(attended.reshape(here * length, span), "cache", axis=0, tiled=True)
-    partial = jnp.dot(rows, out_weight, preferred_element_type=jnp.float32)
-    summed = lax.psum_scatter(
-        partial.astype(jnp.bfloat16), "tensor", scatter_dimension=0, tiled=True
-    )
+    me = me_cache.reshape(1).astype(jnp.int32)
+    lists = jnp.stack([passage_ids, passage_offsets], 1).astype(jnp.bfloat16)
+    lists = jnp.pad(lists, ((0, 0), (0, EXTRA - 2), (0, span - listed)))
+    sent = jnp.concatenate([question_q, lists], 1)
+
+    gathered = [lax.all_gather(sent[r], "cache", axis=0) for r in range(here)]
+    exchanged, pieces = [], []
+    for r in range(here):
+        q = gathered[r]
+        lists_r = q[:, length : length + 2, :listed].astype(jnp.int32)
+        ids, offsets = lists_r[:, 0].reshape(-1), lists_r[:, 1].reshape(-1)
+        cf, sf = tables(offsets, inverse)
+        o = attend(me, ids, passage_home, q, passage_kv, own[r : r + 1], cq, sq, cf, sf)
+        if exchanged:
+            exchanged[-1], o = lax.optimization_barrier((exchanged[-1], o))
+        parts = [lax.dynamic_index_in_dim(o, me_cache, 0, False)]
+        for k in range(1, caches):
+            block = lax.dynamic_index_in_dim(o, (me_cache + k) % caches, 0, False)
+            parts.append(
+                lax.ppermute(block, "cache", [(c, (c + k) % caches) for c in range(caches)])
+            )
+        exchanged.append(parts)
+    for parts in exchanged:
+        attended = merge(parts, length)
+        rows = lax.all_gather(attended, "cache", axis=0, tiled=True)
+        partial = jnp.dot(rows, out_weight, preferred_element_type=jnp.float32)
+        summed = lax.psum_scatter(
+            partial.astype(jnp.bfloat16), "tensor", scatter_dimension=0, tiled=True
+        )
+        pieces.append(deliver(summed, caches, tensors, me_cache, length))
+    return jnp.stack(pieces)
+
+
+def deliver(summed, caches, tensors, me_cache, tokens):
     fan = caches // tensors
-    tokens = here * length
-    columns = out_weight.shape[1]
+    columns = summed.shape[1]
     blocks = summed.reshape(fan, tokens, columns)
     pieces = []
     for turn_at in range(fan):
@@ -246,13 +264,10 @@
             block = lax.dynamic_index_in_dim(blocks, (turn_at + me_cache) % fan, 0, False)
         pieces.append(lax.ppermute(block, ("cache", "tensor"), pairs))
     if fan == 1:
-        mixed = pieces[0]
-    else:
-        stacked = jnp.stack(pieces)
-        order = (me_cache - jnp.arange(fan)) % fan
-        mixed = jnp.take(stacked, order, axis=0)
-        mixed = jnp.swapaxes(mixed, 0, 1).reshape(tokens, fan * columns)
-    return mixed.reshape(here, length, -1)
+        return pieces[0]
+    order = (me_cache - jnp.arange(fan)) % fan
+    mixed = jnp.take(jnp.stack(pieces), order, axis=0)
+    return jnp.swapaxes(mixed, 0, 1).reshape(tokens, fan * columns)
 
 
 def solution(mesh):

time: 466 us -> 455 us (0.976)
  blocking collectives: 154 us -> 0 us
  waiting for transfers between devices: 238 us -> 296 us
  Pallas kernels: 33.7 us -> 72.8 us
  starting transfers between devices: 5.51 us -> 36.1 us
  matrix products: 13.8 us -> 19.7 us
  local copies, waits for them, and re-layouts: 4.99 us -> 10.5 us
    all_to_all x2 -> x0, blocking collectives: 142 us -> none  [the longest x1 94.5 us: local(): o = lax.all_to_all(o, 'cache', split_axis=0, concat_axis=0, tiled=True)]
    ppermute x1 -> x8, waiting for transfers between devices: 46.6 us -> 107 us  [the longest x6 83.1 us: local(): lax.ppermute(block, 'cache', [(c, (c + k) % caches) for c in range(caches)])]
    pallas_call x1 -> x2, Pallas kernels: 30.2 us -> 68.8 us  [attend(): pl.pallas_call(functools.partial(attend_kernel, ids.shape[0] // requests,...]
    ppermute x1 -> x8, starting transfers between devices: 5.43 us -> 35.7 us  [the longest x6 25.7 us: local(): lax.ppermute(block, 'cache', [(c, (c + k) % caches) for c in range(caches)])]
    all_gather x2 -> x4, waiting for transfers between devices: 149 us -> 134 us  [the longest x2 101 us: local(): gathered = [lax.all_gather(sent[r], 'cache', axis=0) for r in range(here)]]
    reduce_scatter x1 -> x2, waiting for transfers between devices: 42 us -> 54.3 us  [local(): lax.psum_scatter(partial.astype(jnp.bfloat16), 'tensor', scatter_dimensio...]
    all_gather x1 -> x0, blocking collectives: 12.1 us -> none  [local(): lax.all_gather(jnp.stack([passage_ids, passage_offsets]), 'cache', axis=1...]
    dot_general x1 -> x2, matrix products: 13.8 us -> 19.7 us  [local(): partial = jnp.dot(rows, out_weight, preferred_element_type=jnp.float32)]
  transfers between devices with their start and end apart: 4 -> 14, of which waited for: 4 -> 8; matrix products, arithmetic and copies ran while one was open for 1% -> 5% of each run, Pallas kernels for 0% -> 9%
where the time goes in v2:
time: 455 us; the launch traced here: 454 us
  waiting for transfers between devices  296 us (65%)
  Pallas kernels  72.8 us (16%)
  starting transfers between devices  36.1 us (8%)
  matrix products  19.7 us (4%)
  between operations  13.7 us (3%)
  local copies, waits for them, and re-layouts  10.5 us (2%)
  other arithmetic  5.51 us (1%)
    all_gather x2, waiting for transfers between devices, local(): gathered = [lax.all_gather(sent[r], 'cache', axis=0) for r in range(here)]  101 us
    ppermute x6, waiting for transfers between devices, local(): lax.ppermute(block, 'cache', [(c, (c + k) % caches) for c in range(caches)])  83.1 us
    pallas_call x2, Pallas kernels, attend(): pl.pallas_call(functools.partial(attend_kernel, ids.shape[0] // requests,...  68.8 us
    reduce_scatter x2, waiting for transfers between devices, local(): lax.psum_scatter(partial.astype(jnp.bfloat16), 'tensor', scatter_dimensio...  54.3 us
    all_gather x2, waiting for transfers between devices, local(): rows = lax.all_gather(attended, 'cache', axis=0, tiled=True)  33.2 us
    ppermute x6, starting transfers between devices, local(): lax.ppermute(block, 'cache', [(c, (c + k) % caches) for c in range(caches)])  25.7 us
    ppermute x2, waiting for transfers between devices, deliver(): pieces.append(lax.ppermute(block, ('cache', 'tensor'), pairs))  24.1 us
    dot_general x2, matrix products, local(): partial = jnp.dot(rows, out_weight, preferred_element_type=jnp.float32)  19.7 us
  transfers between devices with their start and end apart: 14, of which 8 were waited for; matrix products, arithmetic and copies ran while one was open for 5% of the time, Pallas kernels for 9%

profile of v2, /device:TPU:2, one launch (start us, length us, event | category | flops | bytes accessed | tf_op | source)
XLA Modules:
  0.0 454.3 jit_solution(6197791387806829090)
XLA Ops:
  7.3 1.3 fusion.1
  8.6 1.1 fusion.7
  11.2 50.5 %all-gather.5.cloned.1.call-done.q = bf16[4,144,2048]{2,1,0:T(8,128)(2,1)} async-done(((bf16[1,144,2048]{2,1,0:T(8,128)(2,1)}), bf16[4,144,2048]{2,1,0:T(8,128)(2,1)}) %all-gather.5.cloned.1.call-update) | async-done | bytes 2359312 | tf_op jit(solution)/shard_map/all_gather | solution.py:223
  62.4 50.1 %all-gather.7.cloned.1.call-done.q = bf16[4,144,2048]{2,1,0:T(8,128)(2,1)} async-done(((bf16[1,144,2048]{2,1,0:T(8,128)(2,1)}), bf16[4,144,2048]{2,1,0:T(8,128)(2,1)}) %all-gather.7.cloned.1.call-update) | async-done | bytes 2359312 | tf_op jit(solution)/shard_map/all_gather | solution.py:223
  114.1 1.7 copy-done.1
  115.8 3.4 copy-done.2
  119.1 29.1 %shard_map.73 = bf16[4,144,2048]{2,1,0:T(8,128)(2,1)S(1)} custom-call(s32[1]{0:T(128)} %bitcast.me_ref, s32[32]{0:T(128)S(1)} %reshape_squeeze.8.ids, s32[64]{0:T(128)S(1)} %copy-done.4, bf16[4,144,2048]{2,1,0:T(8,128)(2,1)S(1)} %copy-done.1, bf16[16,2,512,256]{3,2,1,0:T(8,128)(2,1)S(1)} %copy-done.2, bf16[1,2,128,256]{3,2,1,0:T(8,128)(2,1)S(1)} %get-tuple-element.26.own, ...), custom_call_target="tpu_custom_call" | custom-call | flops 8589934592 | bytes 13107200 | tf_op jit(solution)/shard_map/pallas_call | solution.py:143
  148.7 1.9 collective-permute-start
  150.7 3.4 copy-done.3
  154.1 39.7 %shard_map.74 = bf16[4,144,2048]{2,1,0:T(8,128)(2,1)S(1)} custom-call(s32[1]{0:T(128)} %bitcast.me_ref, s32[32]{0:T(128)S(1)} %reshape_squeeze.9.ids, s32[64]{0:T(128)S(1)} %copy-done.4, bf16[4,144,2048]{2,1,0:T(8,128)(2,1)S(1)} %copy-done, bf16[16,2,512,256]{3,2,1,0:T(8,128)(2,1)S(1)} %copy-done.3, bf16[1,2,128,256]{3,2,1,0:T(8,128)(2,1)S(1)} %get-tuple-element.25.own, ...), custom_call_target="tpu_custom_call" | custom-call | flops 8589934592 | bytes 13107200 | tf_op jit(solution)/shard_map/pallas_call | solution.py:143
  193.8 2.0 shard_map.75
  196.1 21.7 %collective-permute-start.5 = (bf16[144,2048]{1,0:T(8,128)(2,1)S(1)}, bf16[144,2048]{1,0:T(8,128)(2,1)S(1)}, u32[]{:S(2)}, u32[]{:S(2)}) collective-permute-start(bf16[144,2048]{1,0:T(8,128)(2,1)S(1)} %get-tuple-element.16), channel_id=1, source_target_pairs={{0,8},{4,12},{8,0},{12,4},{1,9},{5,13},{9,1},{13,5},{2,10},{6,14},... | collective-permute-start | bytes 1769480 | tf_op jit(solution)/shard_map/ppermute | solution.py:237
  217.8 1.9 collective-permute-start.4
  219.7 19.2 %collective-permute-done.6.refs_3_ = bf16[144,2048]{1,0:T(8,128)(2,1)S(1)} collective-permute-done((bf16[144,2048]{1,0:T(8,128)(2,1)S(1)}, bf16[144,2048]{1,0:T(8,128)(2,1)S(1)}, u32[]{:S(2)}, u32[]{:S(2)}) %collective-permute-start.6) | collective-permute-done | bytes 589856 | tf_op jit(solution)/shard_map/ppermute | solution.py:237
  238.9 64.0 %collective-permute-done.5.refs_2_ = bf16[144,2048]{1,0:T(8,128)(2,1)S(1)} collective-permute-done((bf16[144,2048]{1,0:T(8,128)(2,1)S(1)}, bf16[144,2048]{1,0:T(8,128)(2,1)S(1)}, u32[]{:S(2)}, u32[]{:S(2)}) %collective-permute-start.5) | collective-permute-done | bytes 589856 | tf_op jit(solution)/shard_map/ppermute | solution.py:237
  302.8 2.0 shard_map.76
  305.1 9.8 %convolution_convert_fusion.1 = bf16[512,2048]{1,0:T(8,128)(2,1)} fusion(bf16[512,2048]{1,0:T(8,128)(2,1)} %all-gather.9.cloned.1.call-done, bf16[2048,2048]{1,0:T(8,128)(2,1)} %param.13), kind=kOutput, calls=%fused_computation.1 | convolution fusion | flops 4296015872 | bytes 12582912 | tf_op jit(solution)/shard_map/dot_general | solution.py:243
  315.0 33.2 %all-gather.11.cloned.1.call-done = bf16[512,2048]{1,0:T(8,128)(2,1)} async-done(((bf16[128,2048]{1,0:T(8,128)(2,1)}), bf16[512,2048]{1,0:T(8,128)(2,1)}) %all-gather.11.cloned.1.call-update) | async-done | bytes 2097168 | tf_op jit(solution)/shard_map/all_gather | solution.py:242
  348.2 9.9 %convolution_convert_fusion = bf16[512,2048]{1,0:T(8,128)(2,1)} fusion(bf16[512,2048]{1,0:T(8,128)(2,1)} %all-gather.11.cloned.1.call-done, bf16[2048,2048]{1,0:T(8,128)(2,1)} %param.13), kind=kOutput, calls=%fused_computation | convolution fusion | flops 4296015872 | bytes 12582912 | tf_op jit(solution)/shard_map/dot_general | solution.py:243
  358.1 21.5 %reduce-scatter.3.cloned.1.call-done = bf16[128,2048]{1,0:T(8,128)(2,1)} async-done(((bf16[512,2048]{1,0:T(8,128)(2,1)}), bf16[128,2048]{1,0:T(8,128)(2,1)}) %reduce-scatter.3.cloned.1.call-update) | async-done | bytes 524304 | tf_op jit(solution)/shard_map/reduce_scatter | solution.py:244
  379.6 5.4 %collective-permute-start.3 = (bf16[128,2048]{1,0:T(8,128)(2,1)}, bf16[128,2048]{1,0:T(8,128)(2,1)S(1)}, u32[]{:S(2)}, u32[]{:S(2)}) collective-permute-start(bf16[128,2048]{1,0:T(8,128)(2,1)} %reduce-scatter.3.cloned.1.call-done), channel_id=1, source_target_pairs={{0,0},{1,4},{2,8},{3,12},{4,1},{5,5},{6,9},{7,13},{8,2},{9,6},{10,... | collective-permute-start | bytes 1572872 | tf_op jit(solution)/shard_map/ppermute | solution.py:265
  385.0 32.7 %reduce-scatter.5.cloned.1.call-done = bf16[128,2048]{1,0:T(8,128)(2,1)} async-done(((bf16[512,2048]{1,0:T(8,128)(2,1)}), bf16[128,2048]{1,0:T(8,128)(2,1)}) %reduce-scatter.5.cloned.1.call-update) | async-done | bytes 524304 | tf_op jit(solution)/shard_map/reduce_scatter | solution.py:244
  417.7 4.6 %collective-permute-start.7 = (bf16[128,2048]{1,0:T(8,128)(2,1)}, bf16[128,2048]{1,0:T(8,128)(2,1)S(1)}, u32[]{:S(2)}, u32[]{:S(2)}) collective-permute-start(bf16[128,2048]{1,0:T(8,128)(2,1)} %reduce-scatter.5.cloned.1.call-done), channel_id=1, source_target_pairs={{0,0},{1,4},{2,8},{3,12},{4,1},{5,5},{6,9},{7,13},{8,2},{9,6},{10,... | collective-permute-start | bytes 1572872 | tf_op jit(solution)/shard_map/ppermute | solution.py:265
  422.3 24.1 %collective-permute-done.7 = bf16[128,2048]{1,0:T(8,128)(2,1)S(1)} collective-permute-done((bf16[128,2048]{1,0:T(8,128)(2,1)}, bf16[128,2048]{1,0:T(8,128)(2,1)S(1)}, u32[]{:S(2)}, u32[]{:S(2)}) %collective-permute-start.7) | collective-permute-done | bytes 524320 | tf_op jit(solution)/shard_map/ppermute | solution.py:265
  (57 shorter events, 6.4 us)
Async XLA Ops:
  6.5 55.1 %all-gather.5.cloned.1.call-start = ((), (), s32[]{:S(2)}) async-start(), calls=%async_computation.2 | async-start | bytes 2949120 | tf_op jit(solution)/shard_map/all_gather | solution.py:223
  8.6 2.0 copy-start.5
  8.6 105.5 %copy-start.4 = (s32[64]{0:T(128)S(1)}, s32[64]{0:T(128)}, u32[]{:S(2)}) copy-start(s32[64]{0:T(128)} %home.3) | copy-start | bytes 772
  9.8 102.8 %all-gather.7.cloned.1.call-start = ((), (), s32[]{:S(2)}) async-start(), calls=%async_computation.3 | async-start | bytes 2949120 | tf_op jit(solution)/shard_map/all_gather | solution.py:223
  10.6 294.5 %all-gather.9.cloned.1.call-start = ((), (), s32[]{:S(2)}) async-start(), calls=%async_computation.4 | async-start | bytes 2621440 | tf_op jit(solution)/shard_map/all_gather | solution.py:242
  114.1 1.7 copy-start.1
  115.8 3.4 copy-start.2
  148.3 2.4 copy-start
  148.6 45.2 %collective-permute-start.2 = (bf16[144,2048]{1,0:T(8,128)(2,1)S(1)}, bf16[144,2048]{1,0:T(8,128)(2,1)S(1)}, u32[]{:S(2)}, u32[]{:S(2)}) collective-permute-start(bf16[144,2048]{1,0:T(8,128)(2,1)S(1)} %get-tuple-element.19), channel_id=1, source_target_pairs={{0,12},{4,0},{8,4},{12,8},{1,13},{5,1},{9,5},{13,9},{2,14},{6,2},{... | collective-permute-start | bytes 1769480 | tf_op jit(solution)/shard_map/ppermute | solution.py:237
  148.6 45.2 %collective-permute-start.1 = (bf16[144,2048]{1,0:T(8,128)(2,1)S(1)}, bf16[144,2048]{1,0:T(8,128)(2,1)S(1)}, u32[]{:S(2)}, u32[]{:S(2)}) collective-permute-start(bf16[144,2048]{1,0:T(8,128)(2,1)S(1)} %get-tuple-element.20), channel_id=1, source_target_pairs={{0,8},{4,12},{8,0},{12,4},{1,9},{5,13},{9,1},{13,5},{2,10},{6,14},... | collective-permute-start | bytes 1769480 | tf_op jit(solution)/shard_map/ppermute | solution.py:237
  148.7 45.1 %collective-permute-start = (bf16[144,2048]{1,0:T(8,128)(2,1)S(1)}, bf16[144,2048]{1,0:T(8,128)(2,1)S(1)}, u32[]{:S(2)}, u32[]{:S(2)}) collective-permute-start(bf16[144,2048]{1,0:T(8,128)(2,1)S(1)} %get-tuple-element.21), channel_id=1, source_target_pairs={{0,4},{4,8},{8,12},{12,0},{1,5},{5,9},{9,13},{13,1},{2,6},{6,10},{... | collective-permute-start | bytes 1769480 | tf_op jit(solution)/shard_map/ppermute | solution.py:237
  150.7 3.4 copy-start.3
  195.8 152.4 %all-gather.11.cloned.1.call-start = ((), (), s32[]{:S(2)}) async-start(), calls=%async_computation.6 | async-start | bytes 2621440 | tf_op jit(solution)/shard_map/all_gather | solution.py:242
  196.0 42.8 %collective-permute-start.6 = (bf16[144,2048]{1,0:T(8,128)(2,1)S(1)}, bf16[144,2048]{1,0:T(8,128)(2,1)S(1)}, u32[]{:S(2)}, u32[]{:S(2)}) collective-permute-start(bf16[144,2048]{1,0:T(8,128)(2,1)S(1)} %get-tuple-element.15), channel_id=1, source_target_pairs={{0,12},{4,0},{8,4},{12,8},{1,13},{5,1},{9,5},{13,9},{2,14},{6,2},{... | collective-permute-start | bytes 1769480 | tf_op jit(solution)/shard_map/ppermute | solution.py:237
  196.1 106.7 %collective-permute-start.5 = (bf16[144,2048]{1,0:T(8,128)(2,1)S(1)}, bf16[144,2048]{1,0:T(8,128)(2,1)S(1)}, u32[]{:S(2)}, u32[]{:S(2)}) collective-permute-start(bf16[144,2048]{1,0:T(8,128)(2,1)S(1)} %get-tuple-element.16), channel_id=1, source_target_pairs={{0,8},{4,12},{8,0},{12,4},{1,9},{5,13},{9,1},{13,5},{2,10},{6,14},... | collective-permute-start | bytes 1769480 | tf_op jit(solution)/shard_map/ppermute | solution.py:237
  217.8 85.1 %collective-permute-start.4 = (bf16[144,2048]{1,0:T(8,128)(2,1)S(1)}, bf16[144,2048]{1,0:T(8,128)(2,1)S(1)}, u32[]{:S(2)}, u32[]{:S(2)}) collective-permute-start(bf16[144,2048]{1,0:T(8,128)(2,1)S(1)} %get-tuple-element.17), channel_id=1, source_target_pairs={{0,4},{4,8},{8,12},{12,0},{1,5},{5,9},{9,13},{13,1},{2,6},{6,10},{... | collective-permute-start | bytes 1769480 | tf_op jit(solution)/shard_map/ppermute | solution.py:237
  304.8 74.7 %reduce-scatter.3.cloned.1.call-start = ((), (), s32[]{:S(2)}) async-start(), calls=%async_computation.5 | async-start | bytes 2621440 | tf_op jit(solution)/shard_map/reduce_scatter | solution.py:244
  315.0 102.8 %reduce-scatter.5.cloned.1.call-start = ((), (), s32[]{:S(2)}) async-start(), calls=%async_computation.7 | async-start | bytes 2621440 | tf_op jit(solution)/shard_map/reduce_scatter | solution.py:244
  379.6 42.7 %collective-permute-start.3 = (bf16[128,2048]{1,0:T(8,128)(2,1)}, bf16[128,2048]{1,0:T(8,128)(2,1)S(1)}, u32[]{:S(2)}, u32[]{:S(2)}) collective-permute-start(bf16[128,2048]{1,0:T(8,128)(2,1)} %reduce-scatter.3.cloned.1.call-done), channel_id=1, source_target_pairs={{0,0},{1,4},{2,8},{3,12},{4,1},{5,5},{6,9},{7,13},{8,2},{9,6},{10,... | collective-permute-start | bytes 1572872 | tf_op jit(solution)/shard_map/ppermute | solution.py:265
  417.7 28.7 %collective-permute-start.7 = (bf16[128,2048]{1,0:T(8,128)(2,1)}, bf16[128,2048]{1,0:T(8,128)(2,1)S(1)}, u32[]{:S(2)}, u32[]{:S(2)}) collective-permute-start(bf16[128,2048]{1,0:T(8,128)(2,1)} %reduce-scatter.5.cloned.1.call-done), channel_id=1, source_target_pairs={{0,0},{1,4},{2,8},{3,12},{4,1},{5,5},{6,9},{7,13},{8,2},{9,6},{10,... | collective-permute-start | bytes 1572872 | tf_op jit(solution)/shard_map/ppermute | solution.py:265
Sparse Core Ops, SparseCore 0:
  9.9 51.7 all-gather.4
  63.2 49.2 all-gather.6
  195.9 106.1 all-gather.8
  305.0 43.1 all-gather.10
  350.5 29.0 reduce-scatter.2
  382.1 35.5 reduce-scatter.4

commit v3 on v2

--- a/solution.py
+++ b/solution.py
@@ -173,35 +173,37 @@
     )(me, ids, home, q, kv, own, cq, sq, cf, sf)
 
 
-def merge_kernel(*refs):
-    out = refs[-1]
-    parts = refs[:-1]
-    length = out.shape[0]
+def merge_kernel(o, out):
+    count = o.shape[0]
+    length = out.shape[1]
     width = length
-    heads = out.shape[1] // width
+    heads = out.shape[2] // width
     for h in range(heads):
         at = slice(h * width, (h + 1) * width)
         levels = []
-        for o in parts:
-            tail = o[length:, at].astype(jnp.float32)
+        for c in range(count):
+            tail = o[c, 0, length:, at].astype(jnp.float32)
             levels.append(tail[0:1] + tail[1:2] + tail[2:3])
         top = functools.reduce(jnp.maximum, levels)
         shares = [jnp.exp2(level - top) for level in levels]
         total = functools.reduce(jnp.add, shares)
         result = jnp.zeros((length, width), jnp.float32)
-        for o, share in zip(parts, shares):
-            column = jnp.transpose(jnp.broadcast_to(share / total, (width, length)))
-            result += o[:length, at].astype(jnp.float32) * column
-        out[:, at] = result.astype(jnp.bfloat16)
-
-
-def merge(parts, length):
-    rows, span = parts[0].shape
+        for c in range(count):
+            column = jnp.transpose(jnp.broadcast_to(shares[c] / total, (width, length)))
+            result += o[c, 0, :length, at].astype(jnp.float32) * column
+        out[0, :, at] = result.astype(jnp.bfloat16)
+
+
+def merge(o, length):
+    count, requests, rows, span = o.shape
     return pl.pallas_call(
         merge_kernel,
-        out_shape=jax.ShapeDtypeStruct((length, span), jnp.bfloat16),
-        compiler_params=pltpu.CompilerParams(vmem_limit_bytes=48 * 1024 * 1024),
-    )(*parts)
+        grid=(requests,),
+        in_specs=[pl.BlockSpec((count, 1, rows, span), lambda i: (0, i, 0, 0))],
+        out_specs=pl.BlockSpec((1, length, span), lambda i: (i, 0, 0)),
+        out_shape=jax.ShapeDtypeStruct((requests, length, span), jnp.bfloat16),
+        compiler_params=pltpu.CompilerParams(vmem_limit_bytes=40 * 1024 * 1024),
+    )(o)
 
 
 def local(
@@ -220,32 +222,30 @@
     lists = jnp.pad(lists, ((0, 0), (0, EXTRA - 2), (0, span - listed)))
     sent = jnp.concatenate([question_q, lists], 1)
 
-    gathered = [lax.all_gather(sent[r], "cache", axis=0) for r in range(here)]
-    exchanged, pieces = [], []
-    for r in range(here):
-        q = gathered[r]
-        lists_r = q[:, length : length + 2, :listed].astype(jnp.int32)
-        ids, offsets = lists_r[:, 0].reshape(-1), lists_r[:, 1].reshape(-1)
-        cf, sf = tables(offsets, inverse)
-        o = attend(me, ids, passage_home, q, passage_kv, own[r : r + 1], cq, sq, cf, sf)
-        if exchanged:
-            exchanged[-1], o = lax.optimization_barrier((exchanged[-1], o))
-        parts = [lax.dynamic_index_in_dim(o, me_cache, 0, False)]
-        for k in range(1, caches):
-            block = lax.dynamic_index_in_dim(o, (me_cache + k) % caches, 0, False)
-            parts.append(
-                lax.ppermute(block, "cache", [(c, (c + k) % caches) for c in range(caches)])
-            )
-        exchanged.append(parts)
-    for parts in exchanged:
-        attended = merge(parts, length)
-        rows = lax.all_gather(attended, "cache", axis=0, tiled=True)
-        partial = jnp.dot(rows, out_weight, preferred_element_type=jnp.float32)
+    q = lax.all_gather(sent, "cache", axis=0, tiled=True)
+    lists = q[:, length : length + 2, :listed].astype(jnp.int32)
+    ids, offsets = lists[:, 0].reshape(-1), lists[:, 1].reshape(-1)
+    cf, sf = tables(offsets, inverse)
+    o = attend(me, ids, passage_home, q, passage_kv, own, cq, sq, cf, sf)
+    o = lax.all_to_all(o, "cache", split_axis=0, concat_axis=0, tiled=True)
+    attended = merge(o.reshape((caches, here) + o.shape[1:]), length)
+    tokens = here * length
+    rows = lax.all_gather(attended.reshape(tokens, span), "cache", axis=0, tiled=True)
+    parts = 2
+    columns = out_weight.shape[1] // parts
+    pieces = []
+    for i in range(parts):
+        partial = jnp.dot(
+            rows,
+            out_weight[:, i * columns : (i + 1) * columns],
+            preferred_element_type=jnp.float32,
+        )
         summed = lax.psum_scatter(
             partial.astype(jnp.bfloat16), "tensor", scatter_dimension=0, tiled=True
         )
-        pieces.append(deliver(summed, caches, tensors, me_cache, length))
-    return jnp.stack(pieces)
+        pieces.append(deliver(summed, caches, tensors, me_cache, tokens))
+    mixed = jnp.stack(pieces, 2)
+    return mixed.reshape(here, length, -1)
 
 
 def deliver(summed, caches, tensors, me_cache, tokens):
@@ -264,10 +264,9 @@
             block = lax.dynamic_index_in_dim(blocks, (turn_at + me_cache) % fan, 0, False)
         pieces.append(lax.ppermute(block, ("cache", "tensor"), pairs))
     if fan == 1:
-        return pieces[0]
+        return pieces[0][:, None]
     order = (me_cache - jnp.arange(fan)) % fan
-    mixed = jnp.take(jnp.stack(pieces), order, axis=0)
-    return jnp.swapaxes(mixed, 0, 1).reshape(tokens, fan * columns)
+    return jnp.swapaxes(jnp.take(jnp.stack(pieces), order, axis=0), 0, 1)
 
 
 def solution(mesh):

time: 455 us -> 480 us (1.055)
  blocking collectives: 0 us -> 143 us
  waiting for transfers between devices: 296 us -> 246 us
  Pallas kernels: 72.8 us -> 37.5 us
  starting transfers between devices: 36.1 us -> 10.4 us
    all_to_all x0 -> x1, blocking collectives: none -> 143 us  [local(): o = lax.all_to_all(o, 'cache', split_axis=0, concat_axis=0, tiled=True)]
    ppermute x6 -> x0, waiting for transfers between devices: 83.1 us -> none  [local(): lax.ppermute(block, 'cache', [(c, (c + k) % caches) for c in range(caches)])]
    all_gather x4 -> x2, waiting for transfers between devices: 134 us -> 170 us  [the longest x1 89.3 us: local(): q = lax.all_gather(sent, 'cache', axis=0, tiled=True)]
    pallas_call x2 -> x1, Pallas kernels: 68.8 us -> 34 us  [attend(): pl.pallas_call(functools.partial(attend_kernel, ids.shape[0] // requests,...]
    ppermute x6 -> x0, starting transfers between devices: 25.7 us -> none  [local(): lax.ppermute(block, 'cache', [(c, (c + k) % caches) for c in range(caches)])]
    unnamed x14 -> x6, local copies, waits for them, and re-layouts: 8.49 us -> 3.33 us
  transfers between devices with their start and end apart: 14 -> 6, of which waited for: 8 -> 5; matrix products, arithmetic and copies ran while one was open for 5% -> 2% of each run, Pallas kernels for 9% -> 0%
where the time goes in v3:
time: 480 us
  waiting for transfers between devices  246 us (51%)
  blocking collectives  143 us (30%)
  Pallas kernels  37.5 us (8%)
  matrix products  18.6 us (4%)
  between operations  13.2 us (3%)
  starting transfers between devices  10.4 us (2%)
  local copies, waits for them, and re-layouts  6.19 us (1%)
  other arithmetic  4.81 us (1%)
    all_to_all x1, blocking collectives, local(): o = lax.all_to_all(o, 'cache', split_axis=0, concat_axis=0, tiled=True)  143 us
    all_gather x1, waiting for transfers between devices, local(): q = lax.all_gather(sent, 'cache', axis=0, tiled=True)  89.3 us
    all_gather x1, waiting for transfers between devices, local(): lax.all_gather(attended.reshape(tokens, span), 'cache', axis=0, tiled=True)  80.9 us
    reduce_scatter x2, waiting for transfers between devices, local(): lax.psum_scatter(partial.astype(jnp.bfloat16), 'tensor', scatter_dimensio...  52 us
    pallas_call x1, Pallas kernels, attend(): pl.pallas_call(functools.partial(attend_kernel, ids.shape[0] // requests,...  34 us
    ppermute x2, waiting for transfers between devices, deliver(): pieces.append(lax.ppermute(block, ('cache', 'tensor'), pairs))  24.1 us
    dot_general x2, matrix products, local(): jnp.dot(rows, out_weight[:, i * columns:(i + 1) * columns], preferred_ele...  18.6 us
    ppermute x2, starting transfers between devices, deliver(): pieces.append(lax.ppermute(block, ('cache', 'tensor'), pairs))  10 us
  transfers between devices with their start and end apart: 6, of which 5 were waited for; matrix products, arithmetic and copies ran while one was open for 2% of the time, Pallas kernels for 0%

profile of v3, /device:TPU:2, one launch (start us, length us, event | category | flops | bytes accessed | tf_op | source)
XLA Modules:
  0.0 479.9 jit_solution(9922366805777812248)
XLA Ops:
  6.5 0.7 convert_bitcast_fusion
  7.3 2.4 fusion.11
  9.8 1.0 copy.20
  10.8 0.3 fusion.12
  11.1 0.1 pad_maximum_fusion.1
  11.2 89.3 %all-gather.3.cloned.1.call-done.q = bf16[8,144,2048]{2,1,0:T(8,128)(2,1)} async-done(((bf16[2,144,2048]{2,1,0:T(8,128)(2,1)}), bf16[8,144,2048]{2,1,0:T(8,128)(2,1)}) %all-gather.3.cloned.1.call-update) | async-done | bytes 4718608 | tf_op jit(solution)/shard_map/all_gather | solution.py:225
  100.6 0.7 slice_convert_fusion.1
  101.5 0.2 fusion.13
  101.9 2.3 copy-done
  104.2 34.0 %shard_map.73 = bf16[8,144,2048]{2,1,0:T(8,128)(2,1)S(1)} custom-call(s32[1]{0:T(128)} %bitcast.me_ref, s32[64]{0:T(128)S(1)} %reshape_squeeze.4.ids, s32[64]{0:T(128)S(1)} %copy-done.1, bf16[8,144,2048]{2,1,0:T(8,128)(2,1)S(1)} %copy-done, bf16[16,2,512,256]{3,2,1,0:T(8,128)(2,1)} %kv.1, bf16[2,2,128,256]{3,2,1,0:T(8,128)(2,1)S(1)} %bitcast.17, ...), custom_call_target="tpu_custom_call" | custom-call | flops 17179869184 | bytes 17825792 | tf_op jit(solution)/shard_map/pallas_call | solution.py:143
  138.2 142.9 %all_to_all.5 = bf16[8,144,2048]{2,1,0:T(8,128)(2,1)S(1)} all-to-all(bf16[8,144,2048]{2,1,0:T(8,128)(2,1)S(1)} %shard_map.73), channel_id=1, replica_groups=mesh['groups'=2,'cache'=4,'tensor'=4] {'cache'}, dimensions={0} | all-to-all | bytes 9437184 | tf_op jit(solution)/shard_map/all_to_all | solution.py:230
  281.1 3.5 shard_map.74
  284.6 80.9 %all-gather.5.cloned.1.call-done = bf16[1024,2048]{1,0:T(8,128)(2,1)} async-done(((bf16[256,2048]{1,0:T(8,128)(2,1)}), bf16[1024,2048]{1,0:T(8,128)(2,1)}) %all-gather.5.cloned.1.call-update) | async-done | bytes 4194320 | tf_op jit(solution)/shard_map/all_gather | solution.py:233
  365.5 9.3 %fusion.8 = bf16[1024,1024]{1,0:T(8,128)(2,1)} fusion(bf16[1024,2048]{1,0:T(8,128)(2,1)} %all-gather.5.cloned.1.call-done, bf16[2048,2048]{1,0:T(8,128)(2,1)} %param.13), kind=kOutput, calls=%fused_computation.7 | convolution fusion | flops 4296015872 | bytes 10485760 | tf_op jit(solution)/shard_map/dot_general | solution.py:238
  374.8 0.2 reduce-scatter.3.cloned.1.call-start
  375.0 9.3 %fusion.5 = bf16[1024,1024]{1,0:T(8,128)(2,1)} fusion(bf16[1024,2048]{1,0:T(8,128)(2,1)} %all-gather.5.cloned.1.call-done, bf16[2048,2048]{1,0:T(8,128)(2,1)} %param.13), kind=kOutput, calls=%fused_computation.6 | convolution fusion | flops 4296015872 | bytes 10485760 | tf_op jit(solution)/shard_map/dot_general | solution.py:238
  384.3 19.4 %reduce-scatter.5.cloned.1.call-done = bf16[256,1024]{1,0:T(8,128)(2,1)} async-done(((bf16[1024,1024]{1,0:T(8,128)(2,1)}), bf16[256,1024]{1,0:T(8,128)(2,1)}) %reduce-scatter.5.cloned.1.call-update) | async-done | bytes 524304 | tf_op jit(solution)/shard_map/reduce_scatter | solution.py:243
  403.7 5.5 %collective-permute-start.1 = (bf16[256,1024]{1,0:T(8,128)(2,1)}, bf16[256,1024]{1,0:T(8,128)(2,1)S(1)}, u32[]{:S(2)}, u32[]{:S(2)}) collective-permute-start(bf16[256,1024]{1,0:T(8,128)(2,1)} %reduce-scatter.5.cloned.1.call-done), channel_id=1, source_target_pairs={{0,0},{1,4},{2,8},{3,12},{4,1},{5,5},{6,9},{7,13},{8,2},{9,6},{10,... | collective-permute-start | bytes 1572872 | tf_op jit(solution)/shard_map/ppermute | solution.py:265
  409.2 32.7 %reduce-scatter.3.cloned.1.call-done = bf16[256,1024]{1,0:T(8,128)(2,1)} async-done(((bf16[1024,1024]{1,0:T(8,128)(2,1)}), bf16[256,1024]{1,0:T(8,128)(2,1)}) %reduce-scatter.3.cloned.1.call-update) | async-done | bytes 524304 | tf_op jit(solution)/shard_map/reduce_scatter | solution.py:243
  441.8 4.6 collective-permute-start
  446.4 24.1 %collective-permute-done = bf16[256,1024]{1,0:T(8,128)(2,1)S(1)} collective-permute-done((bf16[256,1024]{1,0:T(8,128)(2,1)}, bf16[256,1024]{1,0:T(8,128)(2,1)S(1)}, u32[]{:S(2)}, u32[]{:S(2)}) %collective-permute-start) | collective-permute-done | bytes 524320 | tf_op jit(solution)/shard_map/ppermute | solution.py:265
  470.6 0.1 pad_maximum_fusion
  470.7 1.1 copy.17
  471.8 1.6 reshape.47
  (21 shorter events, 0.6 us)
Async XLA Ops:
  6.5 95.3 %copy-start.1 = (s32[64]{0:T(128)S(1)}, s32[64]{0:T(128)}, u32[]{:S(2)}) copy-start(s32[64]{0:T(128)} %home.1) | copy-start | bytes 772
  6.5 94.0 %all-gather.3.cloned.1.call-start = ((), (), s32[]{:S(2)}) async-start(), calls=%async_computation.3 | async-start | bytes 5898240 | tf_op jit(solution)/shard_map/all_gather | solution.py:225
  9.7 355.7 %all-gather.5.cloned.1.call-start = ((), (), s32[]{:S(2)}) async-start(), calls=%async_computation.4 | async-start | bytes 5242880 | tf_op jit(solution)/shard_map/all_gather | solution.py:233
  101.9 2.3 copy-start
  284.6 119.1 %reduce-scatter.5.cloned.1.call-start = ((), (), s32[]{:S(2)}) async-start(), calls=%async_computation.6 | async-start | bytes 2621440 | tf_op jit(solution)/shard_map/reduce_scatter | solution.py:243
  374.8 67.1 %reduce-scatter.3.cloned.1.call-start = ((), (), s32[]{:S(2)}) async-start(), calls=%async_computation.5 | async-start | bytes 2621440 | tf_op jit(solution)/shard_map/reduce_scatter | solution.py:243
  403.7 42.8 %collective-permute-start.1 = (bf16[256,1024]{1,0:T(8,128)(2,1)}, bf16[256,1024]{1,0:T(8,128)(2,1)S(1)}, u32[]{:S(2)}, u32[]{:S(2)}) collective-permute-start(bf16[256,1024]{1,0:T(8,128)(2,1)} %reduce-scatter.5.cloned.1.call-done), channel_id=1, source_target_pairs={{0,0},{1,4},{2,8},{3,12},{4,1},{5,5},{6,9},{7,13},{8,2},{9,6},{10,... | collective-permute-start | bytes 1572872 | tf_op jit(solution)/shard_map/ppermute | solution.py:265
  441.8 28.7 %collective-permute-start = (bf16[256,1024]{1,0:T(8,128)(2,1)}, bf16[256,1024]{1,0:T(8,128)(2,1)S(1)}, u32[]{:S(2)}, u32[]{:S(2)}) collective-permute-start(bf16[256,1024]{1,0:T(8,128)(2,1)} %reduce-scatter.3.cloned.1.call-done), channel_id=1, source_target_pairs={{0,0},{1,4},{2,8},{3,12},{4,1},{5,5},{6,9},{7,13},{8,2},{9,6},{10,... | collective-permute-start | bytes 1572872 | tf_op jit(solution)/shard_map/ppermute | solution.py:265
Sparse Core Ops, SparseCore 0:
  9.9 90.6 all-gather.2
  284.7 80.7 all-gather.4
  374.9 28.7 reduce-scatter.4
  406.2 35.5 reduce-scatter.2

commit v4 on v1

--- a/solution.py
+++ b/solution.py
@@ -208,10 +208,15 @@
     width = passage_kv.shape[-1] // 2
     listed = passage_ids.shape[1]
     inverse = frequencies(width)
-    lists = lax.all_gather(
-        jnp.stack([passage_ids, passage_offsets]), "cache", axis=1, tiled=True
-    )
-    ids, offsets = lists[0].reshape(-1), lists[1].reshape(-1)
+    lists = jnp.stack([passage_ids.reshape(-1), passage_offsets.reshape(-1)])
+    turned = [lists]
+    for k in range(1, caches):
+        turned.append(
+            lax.ppermute(lists, "cache", [(c, (c + k) % caches) for c in range(caches)])
+        )
+    order = (me_cache - jnp.arange(caches)) % caches
+    lists = jnp.take(jnp.stack(turned), order, axis=0)
+    ids, offsets = lists[:, 0].reshape(-1), lists[:, 1].reshape(-1)
     q_all = lax.all_gather(question_q, "cache", axis=0, tiled=True)
     cq, sq = tables(listed * passage_kv.shape[2] + jnp.arange(length), inverse)
     cf, sf = tables(offsets, inverse)

time: 466 us -> 466 us (level)
  blocking collectives: 154 us -> 132 us
  Pallas kernels: 33.7 us -> 44 us
  starting transfers between devices: 5.51 us -> 12 us
    all_gather x1 -> x0, blocking collectives: 12.1 us -> none  [local(): lax.all_gather(jnp.stack([passage_ids, passage_offsets]), 'cache', axis=1...]
    all_to_all x1, blocking collectives: 47.7 us -> 37.3 us  [local(): lse = lax.all_to_all(lse, 'cache', split_axis=0, concat_axis=0, tiled=True)]
    pallas_call x1, Pallas kernels: 30.2 us -> 40.5 us  [attend(): pl.pallas_call(functools.partial(attend_kernel, ids.shape[0] // requests,...]
    ppermute x0 -> x3, starting transfers between devices: none -> 6.47 us  [local(): lax.ppermute(lists, 'cache', [(c, (c + k) % caches) for c in range(caches)])]
  transfers between devices with their start and end apart: 4 -> 7, of which waited for: 4 -> 4; matrix products, arithmetic and copies ran while one was open for 1% -> 1% of each run, Pallas kernels for 0% -> 0%
where the time goes in v4:
time: 466 us; the launch traced here: 465 us
  waiting for transfers between devices  242 us (52%)
  blocking collectives  132 us (28%)
  Pallas kernels  44 us (9%)
  matrix products  13.8 us (3%)
  between operations  13.2 us (3%)
  starting transfers between devices  12 us (3%)
  local copies, waits for them, and re-layouts  7.07 us (2%)
    all_to_all x1, blocking collectives, local(): o = lax.all_to_all(o, 'cache', split_axis=0, concat_axis=0, tiled=True)  94.5 us
    all_gather x1, waiting for transfers between devices, local(): lax.all_gather(attended.reshape(here * length, span), 'cache', axis=0, ti...  80.1 us
    all_gather x1, waiting for transfers between devices, local(): q_all = lax.all_gather(question_q, 'cache', axis=0, tiled=True)  73 us
    ppermute x1, waiting for transfers between devices, local(): pieces.append(lax.ppermute(block, ('cache', 'tensor'), pairs))  46.6 us
    reduce_scatter x1, waiting for transfers between devices, local(): lax.psum_scatter(partial.astype(jnp.bfloat16), 'tensor', scatter_dimensio...  42 us
    pallas_call x1, Pallas kernels, attend(): pl.pallas_call(functools.partial(attend_kernel, ids.shape[0] // requests,...  40.5 us
    all_to_all x1, blocking collectives, local(): lse = lax.all_to_all(lse, 'cache', split_axis=0, concat_axis=0, tiled=True)  37.3 us
    dot_general x1, matrix products, local(): partial = jnp.dot(rows, out_weight, preferred_element_type=jnp.float32)  13.8 us
  transfers between devices with their start and end apart: 7, of which 4 were waited for; matrix products, arithmetic and copies ran while one was open for 1% of the time, Pallas kernels for 0%

profile of v4, /device:TPU:2, one launch (start us, length us, event | category | flops | bytes accessed | tf_op | source)
XLA Modules:
  0.0 465.2 jit_solution(1844123286444083670)
XLA Ops:
  6.5 0.7 all-gather.3.cloned.1.call-update
  7.3 0.8 stack_reshape.6
  8.1 0.8 stack_reshape.7
  8.8 2.6 collective-permute-start.1
  11.5 1.6 collective-permute-start
  13.1 2.2 collective-permute-start.2
  15.4 0.3 fusion
  15.7 0.1 pad_maximum_fusion
  15.8 1.0 copy.11
  16.9 0.6 gather_fusion
  17.7 0.2 fusion.1
  18.0 73.0 %all-gather.3.cloned.1.call-done.q = bf16[8,128,2048]{2,1,0:T(8,128)(2,1)} async-done(((bf16[2,128,2048]{2,1,0:T(8,128)(2,1)}), bf16[8,128,2048]{2,1,0:T(8,128)(2,1)}) %all-gather.3.cloned.1.call-update) | async-done | bytes 4194320 | tf_op jit(solution)/shard_map/all_gather | solution.py:220
  91.0 2.2 copy-done
  93.2 0.7 copy-done.1
  93.9 40.5 %shard_map.73 = (bf16[8,128,2048]{2,1,0:T(8,128)(2,1)S(1)}, f32[8,16,128]{2,1,0:T(8,128)S(1)}) custom-call(s32[1]{0:T(128)} %bitcast.me_ref, s32[64]{0:T(128)S(1)} %reshape_squeeze.4.ids, s32[64]{0:T(128)S(1)} %copy-done.1, bf16[8,128,2048]{2,1,0:T(8,128)(2,1)S(1)} %copy-done, bf16[16,2,512,256]{3,2,1,0:T(8,128)(2,1)} %kv.1, ...), custom_call_target="tpu_custom_call" | custom-call | tf_op jit(solution)/shard_map/pallas_call | solution.py:135
  134.4 37.3 %all_to_all.10 = f32[8,16,128]{2,1,0:T(8,128)S(1)} all-to-all(f32[8,16,128]{2,1,0:T(8,128)S(1)} %get-tuple-element.8), channel_id=1, replica_groups=mesh['groups'=2,'cache'=4,'tensor'=4] {'cache'}, dimensions={0} | all-to-all | bytes 131072 | tf_op jit(solution)/shard_map/all_to_all | solution.py:229
  171.7 94.5 %all_to_all.11 = bf16[8,128,2048]{2,1,0:T(8,128)(2,1)S(1)} all-to-all(bf16[8,128,2048]{2,1,0:T(8,128)(2,1)S(1)} %get-tuple-element.7), channel_id=1, replica_groups=mesh['groups'=2,'cache'=4,'tensor'=4] {'cache'}, dimensions={0} | all-to-all | bytes 8388608 | tf_op jit(solution)/shard_map/all_to_all | solution.py:228
  266.2 3.4 shard_map.74
  269.7 80.1 %all-gather.5.cloned.1.call-done = bf16[1024,2048]{1,0:T(8,128)(2,1)} async-done(((bf16[256,2048]{1,0:T(8,128)(2,1)}), bf16[1024,2048]{1,0:T(8,128)(2,1)}) %all-gather.5.cloned.1.call-update) | async-done | bytes 4194320 | tf_op jit(solution)/shard_map/all_gather | solution.py:233
  349.8 13.8 %convolution_convert_fusion = bf16[1024,2048]{1,0:T(8,128)(2,1)} fusion(bf16[1024,2048]{1,0:T(8,128)(2,1)} %all-gather.5.cloned.1.call-done, bf16[2048,2048]{1,0:T(8,128)(2,1)} %param.13), kind=kOutput, calls=%fused_computation.1 | convolution fusion | flops 8592031744 | bytes 16777216 | tf_op jit(solution)/shard_map/dot_general | solution.py:234
  363.6 42.0 %reduce-scatter.2.cloned.1.call-done = bf16[256,2048]{1,0:T(8,128)(2,1)} async-done(((bf16[1024,2048]{1,0:T(8,128)(2,1)}), bf16[256,2048]{1,0:T(8,128)(2,1)}) %reduce-scatter.2.cloned.1.call-update) | async-done | bytes 1048592 | tf_op jit(solution)/shard_map/reduce_scatter | solution.py:235
  405.6 5.5 %collective-permute-start.3 = (bf16[256,2048]{1,0:T(8,128)(2,1)}, bf16[256,2048]{1,0:T(8,128)(2,1)S(1)}, u32[]{:S(2)}, u32[]{:S(2)}) collective-permute-start(bf16[256,2048]{1,0:T(8,128)(2,1)} %reduce-scatter.2.cloned.1.call-done), channel_id=1, source_target_pairs={{0,0},{1,4},{2,8},{3,12},{4,1},{5,5},{6,9},{7,13},{8,2},{9,6},{10,... | collective-permute-start | bytes 3145736 | tf_op jit(solution)/shard_map/ppermute | solution.py:252
  411.1 46.6 %collective-permute-done.3 = bf16[256,2048]{1,0:T(8,128)(2,1)S(1)} collective-permute-done((bf16[256,2048]{1,0:T(8,128)(2,1)}, bf16[256,2048]{1,0:T(8,128)(2,1)S(1)}, u32[]{:S(2)}, u32[]{:S(2)}) %collective-permute-start.3) | collective-permute-done | bytes 1048608 | tf_op jit(solution)/shard_map/ppermute | solution.py:252
  457.7 1.0 copy.13
  (23 shorter events, 0.6 us)
Async XLA Ops:
  6.5 84.5 %all-gather.3.cloned.1.call-start = ((), (), s32[]{:S(2)}) async-start(), calls=%async_computation.3 | async-start | bytes 5242880 | tf_op jit(solution)/shard_map/all_gather | solution.py:220
  7.3 342.5 %all-gather.5.cloned.1.call-start = ((), (), s32[]{:S(2)}) async-start(), calls=%async_computation.4 | async-start | bytes 5242880 | tf_op jit(solution)/shard_map/all_gather | solution.py:233
  8.8 8.0 %collective-permute-start.1 = (s32[2,16]{1,0:T(2,128)S(1)}, s32[2,16]{1,0:T(2,128)S(1)}, u32[]{:S(2)}, u32[]{:S(2)}) collective-permute-start(s32[2,16]{1,0:T(2,128)S(1)} %get-tuple-element.16), channel_id=1, source_target_pairs={{0,8},{4,12},{8,0},{12,4},{1,9},{5,13},{9,1},{13,5},{2,10},{6,14},... | collective-permute-start | bytes 392 | tf_op jit(solution)/shard_map/ppermute | solution.py:215
  11.5 5.4 %collective-permute-start = (s32[2,16]{1,0:T(2,128)S(1)}, s32[2,16]{1,0:T(2,128)S(1)}, u32[]{:S(2)}, u32[]{:S(2)}) collective-permute-start(s32[2,16]{1,0:T(2,128)S(1)} %get-tuple-element.16), channel_id=1, source_target_pairs={{0,4},{4,8},{8,12},{12,0},{1,5},{5,9},{9,13},{13,1},{2,6},{6,10},{... | collective-permute-start | bytes 392 | tf_op jit(solution)/shard_map/ppermute | solution.py:215
  13.1 3.8 collective-permute-start.2
  91.0 2.2 copy-start
  93.2 0.7 copy-start.1
  269.7 135.9 %reduce-scatter.2.cloned.1.call-start = ((), (), s32[]{:S(2)}) async-start(), calls=%async_computation.5 | async-start | bytes 5242880 | tf_op jit(solution)/shard_map/reduce_scatter | solution.py:235
  405.6 52.1 %collective-permute-start.3 = (bf16[256,2048]{1,0:T(8,128)(2,1)}, bf16[256,2048]{1,0:T(8,128)(2,1)S(1)}, u32[]{:S(2)}, u32[]{:S(2)}) collective-permute-start(bf16[256,2048]{1,0:T(8,128)(2,1)} %reduce-scatter.2.cloned.1.call-done), channel_id=1, source_target_pairs={{0,0},{1,4},{2,8},{3,12},{4,1},{5,5},{6,9},{7,13},{8,2},{9,6},{10,... | collective-permute-start | bytes 3145736 | tf_op jit(solution)/shard_map/ppermute | solution.py:252
Sparse Core Ops, SparseCore 0:
  8.9 82.0 all-gather.2
  269.8 79.9 all-gather.4
  363.7 41.8 reduce-scatter.1
